TPU v7x, 256 devices: a whole 4x4x8 slice. The times are simulated.
256 devices in a mesh: dp: 32 (over x_hi, z, core), tensor: 8 (over y, x_lo).
Axes of the slice: x: 4 (x_hi: 2, x_lo: 2; x = x_hi * 2 + x_lo), y: 4, z: 8, core: 2. Of those that a mesh axis runs over, the one named last changes fastest.
Arguments:
- activations: bfloat16 [16384, 6144], P('dp', 'tensor'), may hold values from -12 to 12
- out_grads: bfloat16 [16384, 3072], P('dp'), may hold values from -6 to 6
- a_basis: bfloat16 [6144, 768], P('tensor'), may hold values from -0.21875 to 0.21875
- a_values: float32 [6144], P('tensor'), may hold values from 0.3 to 3
- g_basis: bfloat16 [3072, 3072], P(None, 'dp'), may hold values from -0.109375 to 0.109375
- g_values: float32 [3072], P('dp'), may hold values from 0.3 to 3
- owners: int32 [2, 32], replicated, may hold values from 0 to 31, each once within a row
- a_factors: float32 [768, 6144], P('dp', 'tensor'), may hold values from -3 to 3
- g_factors: float32 [3072, 3072], P('dp', 'tensor'), may hold values from -3 to 3
Outputs:
- update: float32 [3072, 6144], P('dp', 'tensor')
- new_a_factors: float32 [768, 6144], P('dp', 'tensor')
- new_g_factors: float32 [3072, 3072], P('dp', 'tensor')
Inputs may be any that keep to these rules, and one draw needn't show every extreme that they name: Each row of owners names every worker exactly once.
All inputs are finite; a program needn't handle non-finite values.
Results may differ from a plain program's by a relative error of at most 0.03.
Values may be sent and summed in bfloat16 or wider, within the bound.
A program may use at most 128 MiB of HBM per device.

v0:
```python
import jax
import jax.numpy as jnp
from jax import lax
from jax.sharding import PartitionSpec as P

FEAT = 6144
OUT_WIN = 3072


decay_rate = 0.5
damping = 0.1


def owned_block(order_row, worker, count):
    indices = jnp.arange(count, dtype=jnp.int32)
    return jnp.sum(jnp.where(order_row == worker, indices, 0))


def per_device(
    activations, out_grads, a_basis, a_values, g_basis, g_values, owners, a_factors, g_factors
):
    dp_count = lax.axis_size("dp")
    worker = lax.axis_index("dp")
    tokens_total = float(activations.shape[0] * dp_count)
    contract = (((0,), (0,)), ((), ()))
    a_partial = (
        lax.dot_general(activations, activations, contract, preferred_element_type=jnp.float32)
        / tokens_total
    )
    width = out_grads.shape[1] // lax.axis_size("tensor")
    g_columns = lax.dynamic_slice_in_dim(out_grads, lax.axis_index("tensor") * width, width, 1)
    g_partial = (
        lax.dot_general(out_grads, g_columns, contract, preferred_element_type=jnp.float32)
        / tokens_total
    )
    a_rows = a_partial.shape[0] // dp_count
    g_rows = g_partial.shape[0] // dp_count
    a_summed, g_summed = (
        lax.psum(a_partial.astype(jnp.bfloat16), "dp").astype(jnp.float32),
        lax.psum(g_partial.astype(jnp.bfloat16), "dp").astype(jnp.float32),
    )
    a_reduced = lax.dynamic_slice_in_dim(
        a_summed, owned_block(owners[0], worker, dp_count) * a_rows, a_rows, 0
    )
    g_reduced = lax.dynamic_slice_in_dim(
        g_summed, owned_block(owners[1], worker, dp_count) * g_rows, g_rows, 0
    )
    new_a_factors = decay_rate * a_factors + (1.0 - decay_rate) * a_reduced
    new_g_factors = decay_rate * g_factors + (1.0 - decay_rate) * g_reduced
    partial_value = lax.dot_general(
        out_grads, activations, contract, preferred_element_type=jnp.float32
    ).astype(jnp.bfloat16)
    summed = lax.psum_scatter(
        partial_value.astype(jnp.float32).astype(jnp.bfloat16),
        "dp",
        scatter_dimension=0,
        tiled=True,
    )
    reduced = jnp.dot(summed, a_basis, preferred_element_type=jnp.float32).astype(jnp.bfloat16)
    basis_rows = g_basis
    project = lax.dot_general(
        basis_rows,
        lax.all_gather(reduced, "dp", axis=0, tiled=True),
        contract,
        preferred_element_type=jnp.float32,
    )
    denom = g_values[:, None] * a_values[None, :] + damping
    scaled = project / denom
    kl_total = lax.psum(jnp.sum(project * scaled), ("dp", "tensor"))
    returned = lax.dot_general(
        scaled.astype(jnp.bfloat16),
        a_basis,
        (((1,), (1,)), ((), ())),
        preferred_element_type=jnp.float32,
    ).astype(jnp.bfloat16)
    basis_rows = g_basis
    precond = lax.psum_scatter(
        jnp.dot(basis_rows, returned, preferred_element_type=jnp.float32).astype(jnp.bfloat16),
        "dp",
        scatter_dimension=0,
        tiled=True,
    ).astype(jnp.float32)
    update = precond * jnp.sqrt(OUT_WIN * FEAT / kl_total)
    return (update, new_a_factors, new_g_factors)


def solution(mesh):
    in_specs = (
        P("dp", "tensor"),
        P("dp", None),
        P("tensor", None),
        P("tensor"),
        P(None, "dp"),
        P("dp"),
        P(),
        P("dp", "tensor"),
        P("dp", "tensor"),
    )
    out_specs = (P("dp", "tensor"), P("dp", "tensor"), P("dp", "tensor"))
    return jax.shard_map(
        per_device, mesh=mesh, in_specs=in_specs, out_specs=out_specs, check_vma=False
    )
```

profile of v0, /device:TPU:1, one launch (start us, length us, event | category | flops | bytes accessed | tf_op | source)
XLA Modules:
  0.0 652.9 jit_solution(14726313240017849523)
XLA Ops:
  7.2 0.0 copy-start
  7.2 0.0 reduce-scatter.5.cloned.1.call-start
  7.2 1.8 copy-done
  9.1 5.4 convolution_convert_fusion.1
  14.5 0.0 reduce-scatter.5.cloned.1.call-update
  14.5 0.0 all-gather.2.cloned.1.call-start
  14.6 130.6 %reduce-scatter.5.cloned.1.call-done = bf16[96,768]{1,0:T(8,128)(2,1)} async-done(((bf16[3072,768]{1,0:T(8,128)(2,1)}), bf16[96,768]{1,0:T(8,128)(2,1)}) %reduce-scatter.5.cloned.1.call-update) | async-done | bytes 147472 | tf_op jit(solution)/shard_map/reduce_scatter | solution.py:53
  145.1 2.4 convolution_convert_fusion.3
  147.5 0.0 all-gather.2.cloned.1.call-update
  147.5 0.0 all-reduce.3.cloned.1.call-start
  147.6 3.2 multiply_convert_fusion.1
  150.8 3.0 fusion.1
  153.8 0.0 all-reduce.3.cloned.1.call-update
  153.8 0.0 reduce-scatter.7.cloned.1.call-start
  153.9 86.1 %all-gather.2.cloned.1.call-done = bf16[3072,768]{1,0:T(8,128)(2,1)} async-done(((bf16[96,768]{1,0:T(8,128)(2,1)}), bf16[3072,768]{1,0:T(8,128)(2,1)}) %all-gather.2.cloned.1.call-update) | async-done | bytes 4718608 | tf_op jit(solution)/shard_map/all_gather | solution.py:63
  240.0 4.0 multiply_reduce_fusion
  244.0 5.5 fusion
  249.6 6.6 %copy.18 = bf16[3072,768]{1,0:T(8,128)(2,1)} copy(bf16[3072,768]{0,1:T(8,128)(2,1)} %fusion) | data formatting | bytes 9437184
  256.2 0.0 reduce-scatter.7.cloned.1.call-update
  256.2 0.6 copy-done.4
  256.9 0.6 fusion.14
  258.8 0.0 copy-done.1
  258.8 0.1 copy.15
  259.0 253.2 %all-reduce.3.cloned.1.call-done = (bf16[768,768]{1,0:T(8,128)(2,1)}, bf16[3072,384]{0,1:T(8,128)(2,1)}) async-done(((bf16[768,768]{1,0:T(8,128)(2,1)}, bf16[3072,384]{0,1:T(8,128)(2,1)}), (bf16[768,768]{1,0:T(8,128)(2,1)}, bf16[3072,384]{0,1:T(8,128)(2,1)})) %all-reduce.3.cloned.1.call-update) | async-done | bytes 3538960 | tf_op jit(solution)/shard_map/psum | solution.py:39
  512.2 1.0 add_multiply_fusion
  513.2 0.8 copy.17
  514.0 1.5 add_multiply_fusion.1
  515.6 80.0 %psum.21 = f32[]{:T(128)} all-reduce(f32[]{:T(128)} %get-tuple-element.13), channel_id=1, replica_groups=mesh['dp'=32,'tensor'=8] {'dp','tensor'}, use_global_device_ids=true, to_apply=%region_3.4 | all-reduce | flops 1 | bytes 8 | tf_op jit(solution)/shard_map/psum | solution.py:69
  596.3 46.5 %reduce-scatter.7.cloned.1.call-done = bf16[96,768]{1,0:T(8,128)(2,1)} async-done(((bf16[3072,768]{1,0:T(8,128)(2,1)}), bf16[96,768]{1,0:T(8,128)(2,1)}) %reduce-scatter.7.cloned.1.call-update) | async-done | bytes 147472
  642.8 1.7 copy.19
  644.5 1.0 convert_multiply_fusion
  645.5 0.9 copy.16
  (6 shorter events, 0.0 us)
Async XLA Ops:
  7.2 1.9 copy-start
  7.2 138.0 %reduce-scatter.5.cloned.1.call-start = ((), (), s32[]{:S(2)}) async-start(), calls=%async_computation.2 | async-start | bytes 4866048 | tf_op jit(solution)/shard_map/reduce_scatter | solution.py:53
  14.5 225.4 %all-gather.2.cloned.1.call-start = ((), (), s32[]{:S(2)}) async-start(), calls=%async_computation.3 | async-start | bytes 4866048 | tf_op jit(solution)/shard_map/all_gather | solution.py:63
  147.5 364.7 %all-reduce.3.cloned.1.call-start = ((), (), s32[]{:S(2)}) async-start(), calls=%async_computation.5 | async-start | bytes 7077888 | tf_op jit(solution)/shard_map/psum | solution.py:39
  153.8 86.2 %copy-start.2 = (f32[768]{0:T(1024)S(1)}, f32[768]{0:T(1024)}, u32[]{:S(2)}) copy-start(f32[768]{0:T(1024)} %param.12) | copy-start | bytes 9220
  153.8 86.2 %copy-start.3 = (f32[96]{0:T(128)S(1)}, f32[96]{0:T(128)}, u32[]{:S(2)}) copy-start(f32[96]{0:T(128)} %param.14) | copy-start | bytes 1156
  153.8 489.0 %reduce-scatter.7.cloned.1.call-start = ((), (), s32[]{:S(2)}) async-start(), calls=%async_computation.4 | async-start | bytes 4866048
  256.2 0.7 copy-start.4
  256.2 2.6 copy-start.1
Sparse Core Ops, SparseCore 0:
  14.6 130.4 reduce-scatter.4
  148.9 91.0 all-gather.1
  242.9 269.2 all-reduce.2
  516.3 126.4 reduce-scatter.6
where the time goes:
time: 657 us; the launch traced here: 653 us
  waiting for transfers between devices  516 us (79%)
  blocking collectives  80 us (12%)
  matrix products  23.6 us (4%)
  between operations  15.9 us (2%)
  local copies, waits for them, and re-layouts  12.7 us (2%)
    psum x1, waiting for transfers between devices, per_device(): lax.psum(a_partial.astype(jnp.bfloat16), 'dp').astype(jnp.float32)  253 us
    reduce_scatter x1, waiting for transfers between devices, per_device(): lax.psum_scatter(partial_value.astype(jnp.float32).astype(jnp.bfloat16),...  131 us
    all_gather x1, waiting for transfers between devices, per_device(): lax.all_gather(reduced, 'dp', axis=0, tiled=True)  86.1 us
    psum x1, blocking collectives, per_device(): kl_total = lax.psum(jnp.sum(project * scaled), ('dp', 'tensor'))  80 us
    unnamed x5, waiting for transfers between devices  46.6 us
  transfers between devices with their start and end apart: 4, of which 4 were waited for; matrix products, arithmetic and copies ran while one was open for 4% of the time, Pallas kernels for 0%

commit v1 on v0

v1 whole, which is shorter than its diff:
```python
import functools

import jax
import jax.numpy as jnp
from jax import lax
from jax.experimental import pallas as pl
from jax.experimental.pallas import tpu as pltpu
from jax.sharding import PartitionSpec as P

FEAT = 6144
OUT_WIN = 3072
TOKENS = 16384
DECAY = 0.5
DAMPING = 0.1
F32 = jnp.float32
BF16 = jnp.bfloat16
MESH = pl.DeviceIdType.MESH

NZ = 8
CC = 384
CH = 192
OB = 384
GW = 96
AW = 24
GR = 144
GL = 80

NT = (((1,), (1,)), ((), ()))
TN = (((0,), (0,)), ((), ()))


def dot(a, b, dims=(((1,), (0,)), ((), ()))):
    return lax.dot_general(a, b, dims, preferred_element_type=F32)


def add_rows(rows, dst, srcs, step=16):
    def body(i, _):
        at = pl.ds(pl.multiple_of(i * step, step), step)
        total = srcs[0](at).astype(F32)
        for src in srcs[1:]:
            total = total + src(at).astype(F32)
        dst(at, total)
        return 0

    lax.fori_loop(0, rows // step, body, 0, unroll=2)


def store(ref):
    def put(at, value):
        ref[at, :] = value.astype(ref.dtype)

    return put


def load(ref, first=0):
    def get(at):
        return ref[pl.ds(first + at.start, at.size), :]

    return get


def kernel(
    acts, grads, qa, avals, gbasis, gvals, inv, afac, gfac,
    update, new_a, new_g,
    qat, apt, own, csend, crecv, msend, mrecv,
    xsend, xrecv, xown, eg, g4, g4p, gv, gvs, ab, proj, scl,
    bown, bsend, brecv, fsend, frecv,
    gramg, grama, gcs, gcr, gxs, gxr, gown, gsend, grecv,
    klbuf, klz, kly, klx, klc,
    c_s, c_r, m_s, m_r, x_s, x_r, e_s, e_r, b_s, b_r, f_s, f_r,
    gc_s, gc_r, gx_s, gx_r, gz_s, gz_r, g4_s, g4_r, gv_s, gv_r,
    klz_s, klz_r, kly_s, kly_r, klx_s, klx_r, klc_s, klc_r, loc,
):
    dp = lax.axis_index("dp")
    tensor = lax.axis_index("tensor")
    core = dp % 2
    z = (dp // 2) % NZ
    xh = dp // (2 * NZ)
    y = tensor // 2
    xl = tensor % 2

    def dev(xh_=xh, z_=z, core_=core, y_=y, xl_=xl):
        return ((xh_ * NZ + z_) * 2 + core_, y_ * 2 + xl_)

    sibling = dev(core_=1 - core)
    partner = dev(xh_=1 - xh)
    partner_sibling = dev(xh_=1 - xh, core_=1 - core)
    ring = (dev(z_=(z + 1) % NZ), dev(z_=(z + NZ - 1) % NZ))
    pending = []

    def remote(src, dst, ss, rs, to):
        return pltpu.make_async_remote_copy(
            src_ref=src, dst_ref=dst, send_sem=ss, recv_sem=rs, device_id=to, device_id_type=MESH
        )

    def send(*args):
        copy = remote(*args)
        copy.start()
        pending.append(copy)
        return copy

    barrier = pltpu.get_barrier_semaphore()

    def greet(to):
        pl.semaphore_signal(barrier, inc=1, device_id=to, device_id_type=MESH)

    greet(sibling)
    greet(partner)
    greet(partner_sibling)
    for k in range(1, NZ):
        greet(dev(z_=(z + k) % NZ))
    for k in range(1, 4):
        greet(dev(y_=(y + k) % 4))
    greet(dev(xl_=1 - xl))
    greet(dev(xh_=1 - xh, xl_=1 - xl))

    for i in range(6):
        qat[128 * i : 128 * (i + 1), :] = qa[:, 128 * i : 128 * (i + 1)].T
    for i in range(2):
        apt[384 * i : 384 * (i + 1), :] = dot(
            qat[384 * i : 384 * (i + 1), :], acts[...], NT
        ).astype(BF16)

    def chunk(k):
        d = (z + k) % NZ
        block = grads[:, pl.ds(pl.multiple_of(d * OB, 128), OB)]
        theirs = pl.ds(pl.multiple_of((1 - core) * CC, CC), CC)
        csend[d] = dot(apt[theirs, :], block).astype(BF16)
        return d, block

    def chunk_send(d):
        return remote(csend.at[d], crecv.at[d], c_s.at[d], c_r.at[d], sibling)

    def chunk_own(d, block):
        mine = pl.ds(pl.multiple_of(core * CC, CC), CC)
        own[d] = dot(apt[mine, :], block)

    d0, block0 = chunk(4)
    pl.semaphore_wait(barrier, 15)
    pending.append(chunk_send(d0))
    pending[-1].start()
    chunk_own(d0, block0)

    me4 = xh * 2 + core
    gvs[...] = jnp.broadcast_to(gvals[...].reshape(1, GW), gvs.shape)
    keep_g = pltpu.make_async_copy(gbasis, g4.at[pl.ds(pl.multiple_of(me4 * GW, GW), GW)], loc.at[0])
    keep_v = pltpu.make_async_copy(gvs, gv.at[me4], loc.at[1])
    keep_g.start()
    keep_v.start()
    send(gbasis, g4.at[pl.ds(pl.multiple_of(me4 * GW, GW), GW)], g4_s.at[0], g4_r.at[0], partner)
    send(gvs, gv.at[me4], gv_s.at[0], gv_r.at[0], partner)
    send(gvs, gv.at[me4], gv_s.at[1], gv_r.at[1], sibling)
    send(gvs, gv.at[me4], gv_s.at[2], gv_r.at[2], partner_sibling)

    def offset(direction, it):
        k = 4 - it
        return k if direction == 0 else (NZ - k) % NZ

    def ring_step(it, parity, own_half, sbuf, rbuf, ss, rs, sizes):
        if parity == 1 and it == 0:
            return
        for direction in range(2):
            half = parity if direction == 0 else 1 - parity
            size = sizes[half]
            d = (z + offset(direction, it)) % NZ
            srcs = list(own_half(d, half))
            rows = pl.ds(0, size)
            if it > parity:
                before = rbuf.at[direction, half, it - 1, rows]
                remote(
                    before, before, ss.at[direction, half, it - 1],
                    rs.at[direction, half, it - 1], ring[direction],
                ).wait_recv()
                srcs.append(load(rbuf.at[direction, half, it - 1]))
            add_rows(size, store(sbuf.at[direction, half, it]), srcs)
            send(
                sbuf.at[direction, half, it, rows], rbuf.at[direction, half, it, rows],
                ss.at[direction, half, it], rs.at[direction, half, it], ring[direction],
            )

    def ring_last(half, rbuf, ss, rs, sizes):
        rows = pl.ds(0, sizes[half])
        for direction in range(2):
            last = rbuf.at[direction, half, 3, rows]
            remote(
                last, last, ss.at[direction, half, 3], rs.at[direction, half, 3], ring[direction]
            ).wait_recv()
        return [load(rbuf.at[0, half, 3]), load(rbuf.at[1, half, 3])]

    main_sizes = (CH, CH)
    back_sizes = (CH // 2, CH // 2)
    gram_sizes = (GL, GR - GL)

    def main_own(d, half):
        return load(own.at[d], half * CH), load(crecv.at[d], half * CH)

    def main_step(it, parity):
        ring_step(it, parity, main_own, msend, mrecv, m_s, m_r, main_sizes)

    def main_chunks(ks):
        for k in ks:
            d, block = chunk(k)
            pending.append(chunk_send(d))
            pending[-1].start()
            chunk_own(d, block)

    def main_wait(ks):
        for k in ks:
            chunk_send((z + k) % NZ).wait_recv()

    def gram_g(first, last):
        mine = grads[:, pl.ds(pl.multiple_of(tensor * OB, 128), OB)]

        def body(i, _):
            at = pl.multiple_of(i * 384, 128)
            part = dot(grads[:, pl.ds(at, 384)], mine, TN)
            gramg[pl.ds(i * 4, 4)] = part.reshape(4, GW, OB)
            return 0

        lax.fori_loop(first, last, body, 0)

    def gram_a():
        def body(i, _):
            at = pl.multiple_of(i * 384, 128)
            part = dot(acts[:, pl.ds(at, 384)], acts[...], TN)
            grama[pl.ds(i * 16, 16)] = part.reshape(16, AW, 2 * CC)
            return 0

        lax.fori_loop(0, 2, body, 0)

    def gram_block(xh_, z_, core_):
        w = (xh_ * NZ + z_) * 2 + core_
        return gramg[inv[1, w]], grama[inv[0, w]]

    def put_block(ref, g_part, a_part):
        ref[0:GW, :] = g_part.astype(ref.dtype)
        tail = jnp.concatenate([a_part[:, 0:384], a_part[:, 384:768]], axis=0)
        ref[GW:GR, :] = tail.astype(ref.dtype)

    def gram_core():
        for turn in range(2):
            other = 1 - xh if turn == 0 else xh

            def body(i, _):
                put_block(gcs.at[turn, i], *gram_block(other, i, 1 - core))
                return 0

            lax.fori_loop(0, NZ, body, 0)
            send(gcs.at[turn], gcr.at[turn], gc_s.at[turn], gc_r.at[turn], sibling)

    def gram_sum(dst, xh_, others):
        def body(i, _):
            put_block(gown.at[i], *gram_block(xh_, i, core))
            add_rows(GR, store(dst.at[i]), [load(gown.at[i])] + [load(o.at[i]) for o in others])
            return 0

        lax.fori_loop(0, NZ, body, 0)

    def gram_x():
        remote(gcs.at[0], gcr.at[0], gc_s.at[0], gc_r.at[0], sibling).wait_recv()
        gram_sum(gxs, 1 - xh, [gcr.at[0]])
        send(gxs, gxr, gx_s.at[0], gx_r.at[0], partner)

    def gram_own():
        remote(gcs.at[1], gcr.at[1], gc_s.at[1], gc_r.at[1], sibling).wait_recv()
        remote(gxs, gxr, gx_s.at[0], gx_r.at[0], partner).wait_recv()
        gram_sum(gown, xh, [gcr.at[1], gxr])

    def gram_half(d, half):
        return (load(gown.at[d], half * GL),)

    def gram_step(it, parity):
        ring_step(it, parity, gram_half, gsend, grecv, gz_s, gz_r, gram_sizes)

    main_chunks((3, 5))
    main_wait((4,))
    main_step(0, 0)
    main_wait((3, 5))
    main_step(1, 1)
    main_chunks((2, 6))
    gram_g(0, 4)
    main_step(1, 0)
    main_wait((2, 6))
    main_step(2, 1)
    main_chunks((1, 7, 0))
    gram_g(4, 8)
    main_step(2, 0)
    main_wait((1, 7, 0))
    main_step(3, 1)
    gram_a()
    gram_core()
    main_step(3, 0)
    gram_x()
    send(gbasis, g4.at[pl.ds(pl.multiple_of(me4 * GW, GW), GW)], g4_s.at[1], g4_r.at[1], sibling)
    p_partner = (1 - xh) * 2 + core
    remote(gbasis, g4.at[pl.ds(pl.multiple_of(me4 * GW, GW), GW)], g4_s.at[0], g4_r.at[0], partner).wait_recv()
    piece = g4.at[pl.ds(pl.multiple_of(p_partner * GW, GW), GW)]
    send(piece, piece, g4_s.at[2], g4_r.at[2], sibling)
    ab[...] = jnp.broadcast_to(avals[...].reshape(1, 2 * CC), (128, 2 * CC)).T

    def main_last(half_static):
        return ring_last(half_static, mrecv, m_s, m_r, main_sizes)

    main_last(0)
    main_last(1)

    def half_srcs(half):
        at = pl.multiple_of(half * CH, CH)
        return [
            load(own.at[z], at), load(crecv.at[z], at),
            load(mrecv.at[0, half, 3]), load(mrecv.at[1, half, 3]),
        ]

    add_rows(CH, store(xsend), half_srcs(1 - xh))
    send(xsend, xrecv, x_s.at[0], x_r.at[0], partner)
    add_rows(CH, store(xown), half_srcs(xh))
    gram_own()
    remote(xsend, xrecv, x_s.at[0], x_r.at[0], partner).wait_recv()
    add_rows(CH, store(eg.at[z]), [load(xown), load(xrecv)])

    HALF = CH // 2

    def gather_copy(direction, half, it):
        b = (z + NZ - it) % NZ if direction == 0 else (z + it) % NZ
        part = eg.at[b, pl.ds(half * HALF, HALF)]
        return remote(
            part, part, e_s.at[direction, half, it], e_r.at[direction, half, it], ring[direction]
        )

    def gather_start(it):
        for half in (0, 1):
            for direction in (0, 1):
                side = half if direction == 0 else 1 - half
                if half == 1 and it == 3:
                    continue
                if it > 0:
                    gather_copy(direction, side, it - 1).wait_recv()
                copy = gather_copy(direction, side, it)
                copy.start()
                pending.append(copy)

    def project(b, first=False):
        part = dot(eg[b], g4[:, pl.ds(pl.multiple_of(b * OB, 128), OB)], NT)
        proj[...] = part if first else proj[...] + part

    gather_start(0)
    gram_step(0, 0)
    gram_step(1, 1)
    keep_g.wait()
    keep_v.wait()
    remote(gbasis, g4.at[pl.ds(pl.multiple_of(me4 * GW, GW), GW)], g4_s.at[1], g4_r.at[1], sibling).wait_recv()
    remote(piece, piece, g4_s.at[2], g4_r.at[2], sibling).wait_recv()
    project(z, True)
    gather_start(1)
    for i in range(NZ):
        for h in range(2):
            to = i * OB + h * CH
            at = h * (OUT_WIN // 2) + i * CH
            g4p[:, to : to + CH] = g4[:, at : at + CH]
    gram_step(1, 0)
    project((z + 1) % NZ)
    project((z + 7) % NZ)
    gather_start(2)
    gram_step(2, 1)
    project((z + 2) % NZ)
    project((z + 6) % NZ)
    gather_start(3)
    gather_copy(0, 1, 2).wait_recv()
    gather_copy(1, 0, 2).wait_recv()
    project((z + 3) % NZ)
    project((z + 5) % NZ)
    gather_copy(0, 0, 3).wait_recv()
    gather_copy(1, 1, 3).wait_recv()
    project((z + 4) % NZ)

    remote(gvs, gv.at[me4], gv_s.at[0], gv_r.at[0], partner).wait_recv()
    remote(gvs, gv.at[me4], gv_s.at[1], gv_r.at[1], sibling).wait_recv()
    remote(gvs, gv.at[me4], gv_s.at[2], gv_r.at[2], partner_sibling).wait_recv()
    j = core * 2 + xh
    g_row = jnp.concatenate([gv[p, 0:1, :] for p in range(4)], axis=1)

    def scale(i, kl):
        at = pl.multiple_of(i * 16, 16)
        value = proj[pl.ds(at, 16), :]
        a_col = ab[pl.ds(pl.multiple_of(j * CH + at, 16), 16), 0:1]
        scaled = value / (a_col * g_row + DAMPING)
        scl[pl.ds(at, 16), :] = scaled.astype(BF16)
        return kl + value * scaled

    kl = lax.fori_loop(0, CH // 16, scale, jnp.zeros((16, OB), F32))
    klbuf[0] = jnp.full((8, 128), jnp.sum(kl), F32)

    def kl_round(stage, count, place, peer, buf, ss, rs):
        out = []
        for k in range(1, count):
            copy = remote(klbuf.at[stage], buf.at[place(0)], ss.at[k], rs.at[place(0)], peer(k))
            copy.start()
            pending.append(copy)
            out.append(
                lambda k=k: remote(
                    klbuf.at[stage], buf.at[place(k)], ss.at[k], rs.at[place(k)], peer(k)
                )
            )

        def finish():
            total = klbuf[stage]
            for k in range(1, count):
                out[k - 1]().wait_recv()
                total = total + buf[place(k)]
            klbuf[stage + 1] = total

        return finish

    kl_z = kl_round(
        0, NZ, lambda k: (z + k) % NZ, lambda k: dev(z_=(z + k) % NZ), klz, klz_s, klz_r
    )

    def back_chunk(k):
        d = (z + k) % NZ
        bown[d] = dot(scl[...], g4p[:, pl.ds(pl.multiple_of(d * OB, 128), OB)])

    def back_own(d, half):
        return (load(bown.at[d], half * HALF),)

    def back_step(it, parity):
        ring_step(it, parity, back_own, bsend, brecv, b_s, b_r, back_sizes)

    back_chunk(4)
    back_step(0, 0)
    back_chunk(3)
    back_chunk(5)
    back_step(1, 1)
    back_chunk(2)
    back_chunk(6)
    back_step(1, 0)
    back_step(2, 1)
    kl_z()
    kl_y = kl_round(
        1, 4, lambda k: (y + k) % 4, lambda k: dev(y_=(y + k) % 4), kly, kly_s, kly_r
    )
    gram_step(2, 0)
    back_chunk(1)
    back_chunk(7)
    back_step(2, 0)
    back_step(3, 1)
    kl_y()
    x_at = xh * 2 + xl
    kl_x = kl_round(
        2, 4,
        lambda k: (xh ^ (k // 2)) * 2 + (xl ^ (k % 2)),
        lambda k: dev(xh_=xh ^ (k // 2), xl_=xl ^ (k % 2)),
        klx, klx_s, klx_r,
    )
    back_chunk(0)
    back_step(3, 0)
    gram_step(3, 1)
    gram_step(3, 0)
    kl_x()
    kl_c = kl_round(
        3, 2, lambda k: core if k == 0 else 1 - core, lambda k: sibling, klc, klc_s, klc_r
    )

    for half in (0, 1):
        srcs = ring_last(half, brecv, b_s, b_r, back_sizes)
        srcs.append(load(bown.at[z], half * HALF))
        at = half * HALF
        add_rows(HALF, store(xown.at[pl.ds(at, HALF)]), srcs)
    turned = xown[...].T.astype(BF16)
    for p in range(4):
        fsend[p] = turned[p * GW : (p + 1) * GW, :]
    mine4 = pltpu.make_async_copy(fsend.at[me4], frecv.at[j], loc.at[2])
    mine4.start()
    places = (
        (sibling, xh * 2 + 1 - core, (1 - core) * 2 + xh),
        (partner, (1 - xh) * 2 + core, core * 2 + 1 - xh),
        (partner_sibling, (1 - xh) * 2 + 1 - core, (1 - core) * 2 + 1 - xh),
    )
    for n in (1, 2, 0):
        to, p, _ = places[n]
        send(fsend.at[p], frecv.at[j], f_s.at[n], f_r.at[n], to)

    for half in (0, 1):
        srcs = ring_last(half, grecv, gz_s, gz_r, gram_sizes)
        srcs.append(load(gown.at[z], half * GL))
        at = half * GL
        size = gram_sizes[half]
        add_rows(size, store(gown.at[(z + 1) % NZ, pl.ds(at, size)]), srcs)
    fresh = (1.0 - DECAY) / TOKENS
    last = gown.at[(z + 1) % NZ]
    new_g[...] = DECAY * gfac[...] + fresh * last[0:GW, :]
    new_a[:, 0:384] = DECAY * afac[:, 0:384] + fresh * last[GW : GW + AW, :]
    new_a[:, 384:768] = DECAY * afac[:, 384:768] + fresh * last[GW + AW : GR, :]

    kl_c()
    gain = jnp.sqrt(OUT_WIN * FEAT / klbuf[4, 0:1, 0:1])
    mine4.wait()
    for n in (0, 1, 2):
        to, p, slot = places[n]
        remote(fsend.at[p], frecv.at[slot], f_s.at[n], f_r.at[n], to).wait_recv()
    total = dot(frecv[0], qat[0:CH, :])
    for i in range(1, 4):
        total = total + dot(frecv[i], qat[i * CH : (i + 1) * CH, :])
    update[...] = total * gain

    for copy in pending:
        copy.wait_send()


def per_device(
    activations, out_grads, a_basis, a_values, g_basis, g_values, owners, a_factors, g_factors
):
    workers = jnp.arange(owners.shape[1], dtype=jnp.int32)
    inverse = jnp.sum(
        jnp.where(owners[:, None, :] == workers[None, :, None], workers[None, None, :], 0), axis=2
    )
    vmem = pl.BlockSpec(memory_space=pltpu.VMEM)
    smem = pl.BlockSpec(memory_space=pltpu.SMEM)
    sem = pltpu.SemaphoreType.DMA
    v = pltpu.VMEM
    scratch = [
        v((768, 768), BF16), v((768, 512), BF16), v((NZ, CC, OB), F32),
        v((NZ, CC, OB), BF16), v((NZ, CC, OB), BF16),
        v((2, 2, 4, CH, OB), BF16), v((2, 2, 4, CH, OB), BF16),
        v((CH, OB), BF16), v((CH, OB), BF16), v((CH, OB), F32),
        v((NZ, CH, OB), BF16), v((4 * GW, OUT_WIN), BF16), v((4 * GW, OUT_WIN), BF16), v((4, 8, GW), F32), v((8, GW), F32),
        v((768, 128), F32), v((CH, OB), F32), v((CH, OB), BF16),
        v((NZ, CH, OB), F32), v((2, 2, 4, CH // 2, OB), BF16), v((2, 2, 4, CH // 2, OB), BF16),
        v((4, GW, CH), BF16), v((4, GW, CH), BF16),
        v((32, GW, OB), F32), v((32, AW, 768), F32),
        v((2, NZ, GR, OB), BF16), v((2, NZ, GR, OB), BF16),
        v((NZ, GR, OB), BF16), v((NZ, GR, OB), BF16), v((NZ, GR, OB), F32),
        v((2, 2, 4, GL, OB), BF16), v((2, 2, 4, GL, OB), BF16),
        v((5, 8, 128), F32), v((NZ, 8, 128), F32), v((4, 8, 128), F32), v((4, 8, 128), F32),
        v((2, 8, 128), F32),
        sem((NZ,)), sem((NZ,)), sem((2, 2, 4)), sem((2, 2, 4)), sem((1,)), sem((1,)),
        sem((2, 2, 4)), sem((2, 2, 4)), sem((2, 2, 4)), sem((2, 2, 4)), sem((3,)), sem((3,)),
        sem((2,)), sem((2,)), sem((1,)), sem((1,)), sem((2, 2, 4)), sem((2, 2, 4)),
        sem((3,)), sem((3,)), sem((3,)), sem((3,)),
        sem((NZ,)), sem((NZ,)), sem((4,)), sem((4,)), sem((4,)), sem((4,)), sem((2,)), sem((2,)),
        sem((3,)),
    ]
    return pl.pallas_call(
        kernel,
        out_shape=(
            jax.ShapeDtypeStruct((GW, 768), F32),
            jax.ShapeDtypeStruct((AW, 768), F32),
            jax.ShapeDtypeStruct((GW, OB), F32),
        ),
        in_specs=[vmem] * 6 + [smem] + [vmem] * 2,
        out_specs=(vmem, vmem, vmem),
        scratch_shapes=scratch,
        compiler_params=pltpu.CompilerParams(
            collective_id=0, has_side_effects=True, vmem_limit_bytes=60 << 20
        ),
        cost_estimate=pl.CostEstimate(
            flops=5_400_000_000, bytes_accessed=8_000_000, transcendentals=0
        ),
        name="precondition",
    )(
        activations, out_grads, a_basis, a_values, g_basis.T,
        g_values, inverse, a_factors, g_factors,
    )


def solution(mesh):
    in_specs = (
        P("dp", "tensor"),
        P("dp", None),
        P("tensor", None),
        P("tensor"),
        P(None, "dp"),
        P("dp"),
        P(),
        P("dp", "tensor"),
        P("dp", "tensor"),
    )
    out_specs = (P("dp", "tensor"), P("dp", "tensor"), P("dp", "tensor"))
    return jax.shard_map(
        per_device, mesh=mesh, in_specs=in_specs, out_specs=out_specs, check_vma=False
    )
```

time: 657 us -> 109 us (0.17)
  waiting for transfers between devices: 516 us -> 0 us
  Pallas kernels: 0 us -> 102 us
  blocking collectives: 80 us -> 0 us
  matrix products: 23.6 us -> 0 us
  between operations: 15.9 us -> 0.64 us
  local copies, waits for them, and re-layouts: 12.7 us -> 4.79 us
    psum x1 -> x0, waiting for transfers between devices: 253 us -> none  [per_device(): lax.psum(a_partial.astype(jnp.bfloat16), 'dp').astype(jnp.float32)]
    reduce_scatter x1 -> x0, waiting for transfers between devices: 131 us -> none  [per_device(): lax.psum_scatter(partial_value.astype(jnp.float32).astype(jnp.bfloat16),...]
    pallas_call x0 -> x1, Pallas kernels: none -> 102 us  [per_device(): pl.pallas_call(kernel, out_shape=(jax.ShapeDtypeStruct((GW, 768), F32), j...]
    all_gather x1 -> x0, waiting for transfers between devices: 86.1 us -> none  [per_device(): lax.all_gather(reduced, 'dp', axis=0, tiled=True)]
    psum x1 -> x0, blocking collectives: 80 us -> none  [per_device(): kl_total = lax.psum(jnp.sum(project * scaled), ('dp', 'tensor'))]
    unnamed x5 -> x0, waiting for transfers between devices: 46.6 us -> none
    dot_general x6 -> x0, matrix products: 23.6 us -> none  [the longest x1 5.55 us: per_device(): jnp.dot(basis_rows, returned, preferred_element_type=jnp.float32)]
    unnamed x15 -> x3, local copies, waits for them, and re-layouts: 12.7 us -> 4.79 us
  transfers between devices with their start and end apart: 4 -> 0, of which waited for: 4 -> 0; matrix products, arithmetic and copies ran while one was open for 4% -> 0% of each run, Pallas kernels for 0% -> 0%
where the time goes in v1:
time: 109 us
  Pallas kernels  102 us (94%)
  local copies, waits for them, and re-layouts  4.79 us (4%)
  other arithmetic  1.36 us (1%)
    pallas_call x1, Pallas kernels, per_device(): pl.pallas_call(kernel, out_shape=(jax.ShapeDtypeStruct((GW, 768), F32), j...  102 us
    unnamed x3, local copies, waits for them, and re-layouts  4.79 us

profile of v1, /device:TPU:1, one launch (start us, length us, event | category | flops | bytes accessed | tf_op | source)
XLA Modules:
  0.0 108.7 jit_solution(11705370340052184289)
XLA Ops:
  0.6 1.4 %select_reduce_fusion.inv = s32[2,32]{1,0:T(2,128)} fusion(s32[2,32]{1,0:T(2,128)} %param.15), kind=kLoop, calls=%fused_computation | loop fusion | flops 6080 | bytes 512 | tf_op jit(solution)/shard_map/reduce_sum | solution.py:513
  2.0 101.9 %precondition.1 = (f32[96,768]{1,0:T(8,128)}, f32[24,768]{1,0:T(8,128)}, f32[96,384]{1,0:T(8,128)}) custom-call(bf16[512,768]{1,0:T(8,128)(2,1)} %acts.1, bf16[512,3072]{1,0:T(8,128)(2,1)} %grads.1, bf16[768,768]{1,0:T(8,128)(2,1)} %qa.1, f32[768]{0:T(1024)} %avals.1, bf16[96,3072]{1,0:T(8,128)(2,1)} %bitcast.1, f32[96]{0:T(128)} %gvals.1, ...), custom_call_target="tpu_custom_call" | custom-call | flops 5400000000 | bytes 8000000 | tf_op jit(solution)/shard_map/precondition/pallas_call | solution.py:542
  103.9 1.7 %copy.15 = f32[96,768]{1,0:T(8,128)} copy(f32[96,768]{1,0:T(8,128)} %get-tuple-element.6) | data formatting | bytes 589824
  105.6 1.5 %copy.16 = f32[24,768]{1,0:T(8,128)} copy(f32[24,768]{1,0:T(8,128)} %get-tuple-element.7) | data formatting | bytes 147456
  107.1 1.6 %copy.17 = f32[96,384]{1,0:T(8,128)} copy(f32[96,384]{1,0:T(8,128)} %get-tuple-element.8) | data formatting | bytes 294912

commit v2 on v1

v2 whole, which is shorter than its diff:
```python
import functools

import jax
import jax.numpy as jnp
from jax import lax
from jax.experimental import pallas as pl
from jax.experimental.pallas import tpu as pltpu
from jax.sharding import PartitionSpec as P

FEAT = 6144
OUT_WIN = 3072
TOKENS = 16384
DECAY = 0.5
DAMPING = 0.1
F32 = jnp.float32
BF16 = jnp.bfloat16
MESH = pl.DeviceIdType.MESH

NZ = 8
CC = 384
HALF = 192
CH = 96
OB = 384
GW = 96
AW = 24
GR = 144
GL = 80

NT = (((1,), (1,)), ((), ()))
TN = (((0,), (0,)), ((), ()))


def dot(a, b, dims=(((1,), (0,)), ((), ()))):
    return lax.dot_general(a, b, dims, preferred_element_type=F32)


def add_rows(rows, dst, srcs, step=16):
    def body(i, _):
        at = pl.ds(pl.multiple_of(i * step, step), step)
        total = srcs[0](at).astype(F32)
        for src in srcs[1:]:
            total = total + src(at).astype(F32)
        dst(at, total)
        return 0

    lax.fori_loop(0, rows // step, body, 0, unroll=2)


def store(ref):
    def put(at, value):
        ref[at, :] = value.astype(ref.dtype)

    return put


def load(ref, first=0):
    def get(at):
        return ref[pl.ds(first + at.start, at.size), :]

    return get


def kernel(
    acts_in, grads_in, qa_in, gbasis_in, avals, gvals, inv,
    total, gram, gain,
    acts, grads, qa, qat, apt, own, csend, crecv,
    asend, arecv, xsend, xrecv, xown, xbs, xbr, bsend, brecv,
    eg, g4, g4p, gv, gvs, ab, proj, scl,
    rown, rsend, rrecv, fsend, frecv,
    gramg, grama, gcs, gcr, gxs, gxr, gown, gsend, grecv,
    klbuf, klz, kly, klx, klc,
    c_s, c_r, a_s, a_r, x_s, x_r, xb_s, xb_r, b_s, b_r, e_s, e_r, r_s, r_r, f_s, f_r,
    gc_s, gc_r, gx_s, gx_r, gz_s, gz_r, gb_s, gb_r, gv_s, gv_r,
    klz_s, klz_r, kly_s, kly_r, klx_s, klx_r, klc_s, klc_r, loc,
):
    dp = lax.axis_index("dp")
    tensor = lax.axis_index("tensor")
    core = dp % 2
    z = (dp // 2) % NZ
    xh = dp // (2 * NZ)
    y = tensor // 2
    xl = tensor % 2

    def dev(xh_=xh, z_=z, core_=core, y_=y, xl_=xl):
        return ((xh_ * NZ + z_) * 2 + core_, y_ * 2 + xl_)

    sibling = dev(core_=1 - core)
    partner = dev(xh_=1 - xh)
    partner_sibling = dev(xh_=1 - xh, core_=1 - core)
    ring = (dev(z_=(z + 1) % NZ), dev(z_=(z + NZ - 1) % NZ))
    pending = []

    def remote(src, dst, ss, rs, to):
        return pltpu.make_async_remote_copy(
            src_ref=src, dst_ref=dst, send_sem=ss, recv_sem=rs, device_id=to, device_id_type=MESH
        )

    def send(*args):
        copy = remote(*args)
        copy.start()
        pending.append(copy)
        return copy

    def drain():
        for copy in pending:
            copy.wait_send()
        pending.clear()

    barrier = pltpu.get_barrier_semaphore()

    def greet(to):
        pl.semaphore_signal(barrier, inc=1, device_id=to, device_id_type=MESH)

    me4 = xh * 2 + core
    mine4 = pl.ds(pl.multiple_of(me4 * GW, GW), GW)
    loads = [
        pltpu.make_async_copy(qa_in, qa, loc.at[0]),
        pltpu.make_async_copy(acts_in, acts, loc.at[1]),
        pltpu.make_async_copy(grads_in, grads, loc.at[2]),
        pltpu.make_async_copy(gbasis_in, g4.at[mine4], loc.at[3]),
    ]
    for copy in loads:
        copy.start()
    greet(sibling)
    greet(partner)
    greet(partner_sibling)
    for k in range(1, NZ):
        greet(dev(z_=(z + k) % NZ))
    for k in range(1, 4):
        greet(dev(y_=(y + k) % 4))
    greet(dev(xl_=1 - xl))
    greet(dev(xh_=1 - xh, xl_=1 - xl))

    loads[0].wait()
    for i in range(6):
        qat[128 * i : 128 * (i + 1), :] = qa[:, 128 * i : 128 * (i + 1)].T
    loads[1].wait()
    for i in range(2):
        apt[384 * i : 384 * (i + 1), :] = dot(
            qat[384 * i : 384 * (i + 1), :], acts[...], NT
        ).astype(BF16)
    loads[2].wait()

    def chunk(k):
        d = (z + k) % NZ
        block = grads[:, pl.ds(pl.multiple_of(d * OB, 128), OB)]
        theirs = pl.ds(pl.multiple_of((1 - core) * CC, CC), CC)
        csend[d] = dot(apt[theirs, :], block).astype(BF16)
        return d, block

    def chunk_send(d):
        return remote(csend.at[d], crecv.at[d], c_s.at[d], c_r.at[d], sibling)

    def chunk_own(d, block):
        mine = pl.ds(pl.multiple_of(core * CC, CC), CC)
        own[d] = dot(apt[mine, :], block)

    d0, block0 = chunk(4)
    loads[3].wait()
    gvs[...] = jnp.broadcast_to(gvals[...].reshape(1, GW), gvs.shape)
    pl.semaphore_wait(barrier, 15)
    pending.append(chunk_send(d0))
    pending[-1].start()

    quarter = OUT_WIN // 4

    def gb_part(p, y_):
        rows = pl.ds(pl.multiple_of(p * GW, GW), GW)
        return g4.at[rows, pl.ds(pl.multiple_of(y_ * quarter, 128), quarter)]

    def gb_all(p):
        return g4.at[pl.ds(pl.multiple_of(p * GW, GW), GW)]

    p_partner = (1 - xh) * 2 + core
    send(gb_part(me4, y), gb_part(me4, y), gb_s.at[0], gb_r.at[y], partner)
    chunk_own(d0, block0)

    def offset(direction, it):
        k = 4 - it
        return k if direction == 0 else (NZ - k) % NZ

    def ring_step(it, parity, own_half, sbuf, rbuf, ss, rs, sizes):
        for direction in range(2):
            half = parity if direction == 0 else 1 - parity
            size = sizes[half]
            d = (z + offset(direction, it)) % NZ
            srcs = list(own_half(d, half))
            rows = pl.ds(0, size)
            if it > parity:
                before = rbuf.at[direction, half, it - 1, rows]
                remote(
                    before, before, ss.at[direction, half, it - 1],
                    rs.at[direction, half, it - 1], ring[direction],
                ).wait_recv()
                srcs.append(load(rbuf.at[direction, half, it - 1]))
            add_rows(size, store(sbuf.at[direction, half, it]), srcs)
            send(
                sbuf.at[direction, half, it, rows], rbuf.at[direction, half, it, rows],
                ss.at[direction, half, it], rs.at[direction, half, it], ring[direction],
            )

    def ring_last(half, rbuf, ss, rs, sizes):
        rows = pl.ds(0, sizes[half])
        for direction in range(2):
            last = rbuf.at[direction, half, 3, rows]
            remote(
                last, last, ss.at[direction, half, 3], rs.at[direction, half, 3], ring[direction]
            ).wait_recv()
        return [load(rbuf.at[0, half, 3]), load(rbuf.at[1, half, 3])]

    a_sizes = (CH, CH)
    part_sizes = (CH // 2, CH // 2)
    gram_sizes = (GL, GR - GL)
    PART = CH // 2

    def chunks(ks):
        for k in ks:
            d, block = chunk(k)
            pending.append(chunk_send(d))
            pending[-1].start()
            chunk_own(d, block)

    def chunks_wait(ks):
        for k in ks:
            chunk_send((z + k) % NZ).wait_recv()

    def a_own(d, half):
        return load(own.at[d], half * CH), load(crecv.at[d], half * CH)

    def a_step(it, parity):
        ring_step(it, parity, a_own, asend, arecv, a_s, a_r, a_sizes)

    def bx_copy(d):
        return remote(xbs.at[d], xbr.at[d], xb_s.at[d], xb_r.at[d], partner)

    def bx_send(ks):
        for k in ks:
            d = (z + k) % NZ
            at = HALF + (1 - xh) * CH
            add_rows(CH, store(xbs.at[d]), [load(own.at[d], at), load(crecv.at[d], at)])
            copy = bx_copy(d)
            copy.start()
            pending.append(copy)

    def bx_wait(ks):
        for k in ks:
            bx_copy((z + k) % NZ).wait_recv()

    def b_own(d, half):
        at = HALF + xh * CH + half * PART
        return load(own.at[d], at), load(crecv.at[d], at), load(xbr.at[d], half * PART)

    def b_step(it, parity):
        ring_step(it, parity, b_own, bsend, brecv, b_s, b_r, part_sizes)

    def gram_g(first, last):
        mine = grads[:, pl.ds(pl.multiple_of(tensor * OB, 128), OB)]

        def body(i, _):
            at = pl.multiple_of(i * 384, 128)
            part = dot(grads[:, pl.ds(at, 384)], mine, TN)
            gramg[pl.ds(i * 4, 4)] = part.reshape(4, GW, OB)
            return 0

        lax.fori_loop(first, last, body, 0)

    def gram_a():
        def body(i, _):
            at = pl.multiple_of(i * 384, 128)
            part = dot(acts[:, pl.ds(at, 384)], acts[...], TN)
            grama[pl.ds(i * 16, 16)] = part.reshape(16, AW, 2 * CC)
            return 0

        lax.fori_loop(0, 2, body, 0)

    def gram_block(xh_, z_, core_):
        w = (xh_ * NZ + z_) * 2 + core_
        return gramg[inv[1, w]], grama[inv[0, w]]

    def put_block(ref, g_part, a_part):
        ref[0:GW, :] = g_part.astype(ref.dtype)
        tail = jnp.concatenate([a_part[:, 0:384], a_part[:, 384:768]], axis=0)
        ref[GW:GR, :] = tail.astype(ref.dtype)

    def gram_core(turn):
        other = 1 - xh if turn == 0 else xh

        def body(i, _):
            put_block(gcs.at[turn, i], *gram_block(other, i, 1 - core))
            return 0

        lax.fori_loop(0, NZ, body, 0)
        send(gcs.at[turn], gcr.at[turn], gc_s.at[turn], gc_r.at[turn], sibling)

    def gram_sum(dst, xh_, others):
        def body(i, _):
            put_block(gown.at[i], *gram_block(xh_, i, core))
            add_rows(GR, store(dst.at[i]), [load(gown.at[i])] + [load(o.at[i]) for o in others])
            return 0

        lax.fori_loop(0, NZ, body, 0)

    def gram_x():
        remote(gcs.at[0], gcr.at[0], gc_s.at[0], gc_r.at[0], sibling).wait_recv()
        gram_sum(gxs, 1 - xh, [gcr.at[0]])
        send(gxs, gxr, gx_s.at[0], gx_r.at[0], partner)

    def gram_own():
        remote(gcs.at[1], gcr.at[1], gc_s.at[1], gc_r.at[1], sibling).wait_recv()
        remote(gxs, gxr, gx_s.at[0], gx_r.at[0], partner).wait_recv()
        gram_sum(gown, xh, [gcr.at[1], gxr])

    def gram_half(d, half):
        return (load(gown.at[d], half * GL),)

    def gram_step(it, parity):
        ring_step(it, parity, gram_half, gsend, grecv, gz_s, gz_r, gram_sizes)

    def gather_copy(s, direction, half, it):
        b = (z + NZ - it) % NZ if direction == 0 else (z + it) % NZ
        part = eg.at[s, b, pl.ds(half * PART, PART)]
        return remote(
            part, part, e_s.at[s, direction, half, it], e_r.at[s, direction, half, it],
            ring[direction],
        )

    def gather(s, it):
        for half in (0, 1):
            for direction in (0, 1):
                side = half if direction == 0 else 1 - half
                if half == 1 and it == 3:
                    continue
                if it > 0:
                    gather_copy(s, direction, side, it - 1).wait_recv()
                copy = gather_copy(s, direction, side, it)
                copy.start()
                pending.append(copy)

    def gather_last(s):
        gather_copy(s, 0, 1, 2).wait_recv()
        gather_copy(s, 1, 0, 2).wait_recv()
        project(s, 3)
        project(s, 5)
        gather_copy(s, 0, 0, 3).wait_recv()
        gather_copy(s, 1, 1, 3).wait_recv()
        project(s, 4)

    def project(s, k):
        b = (z + k) % NZ
        part = dot(eg[s, b], g4[:, pl.ds(pl.multiple_of(b * OB, 128), OB)], NT)
        proj[s] = part if k == 0 else proj[s] + part

    def scale(s):
        g_row = jnp.concatenate([gv[p, 0:1, :] for p in range(4)], axis=1)
        first = core * CC + s * HALF + xh * CH

        def body(i, kl):
            at = pl.multiple_of(i * 16, 16)
            value = proj[s, pl.ds(at, 16), :]
            a_col = ab[pl.ds(pl.multiple_of(first + at, 16), 16), 0:1]
            scaled = value / (a_col * g_row + DAMPING)
            scl[s, pl.ds(at, 16), :] = scaled.astype(BF16)
            return kl + value * scaled

        return lax.fori_loop(0, CH // 16, body, jnp.zeros((16, OB), F32))

    def back_chunks(s, ks):
        for k in ks:
            d = (z + k) % NZ
            rown[s, d] = dot(scl[s], g4p[:, pl.ds(pl.multiple_of(d * OB, 128), OB)])

    def back_step(s, it, parity):
        def back_own(d, half):
            return (load(rown.at[s, d], half * PART),)

        ring_step(
            it, parity, back_own, rsend.at[s], rrecv.at[s], r_s.at[s], r_r.at[s], part_sizes
        )

    places = (
        (sibling, xh * 2 + 1 - core, (1 - core) * 2 + xh),
        (partner, (1 - xh) * 2 + core, core * 2 + 1 - xh),
        (partner_sibling, (1 - xh) * 2 + 1 - core, (1 - core) * 2 + 1 - xh),
    )
    j = core * 2 + xh

    def final_copy(s, n):
        to, p, _ = places[n]
        return remote(fsend.at[s, p], frecv.at[s, j], f_s.at[s, n], f_r.at[s, n], to)

    def final_keep(s):
        return pltpu.make_async_copy(fsend.at[s, me4], frecv.at[s, j], loc.at[4 + s])

    def final_send(s):
        for half in (0, 1):
            srcs = ring_last(half, rrecv.at[s], r_s.at[s], r_r.at[s], part_sizes)
            srcs.append(load(rown.at[s, z], half * PART))
            add_rows(PART, store(xown.at[pl.ds(half * PART, PART)]), srcs)
        turned = xown[...].T.astype(BF16)
        for p in range(4):
            fsend[s, p] = turned[p * GW : (p + 1) * GW, :]
        for n in (1, 2, 0):
            copy = final_copy(s, n)
            copy.start()
            pending.append(copy)
        final_keep(s).start()

    def final_dot(s):
        final_keep(s).wait()
        for n in (0, 1, 2):
            to, p, slot = places[n]
            remote(
                fsend.at[s, p], frecv.at[s, slot], f_s.at[s, n], f_r.at[s, n], to
            ).wait_recv()
        out = None
        for i in range(4):
            first = (i // 2) * CC + s * HALF + (i % 2) * CH
            part = dot(frecv[s, i], qat[first : first + CH, :])
            out = part if out is None else out + part
        return out

    def kl_round(stage, count, place, peer, buf, ss, rs):
        copies = []
        for k in range(1, count):
            send(klbuf.at[stage], buf.at[place(0)], ss.at[k], rs.at[place(0)], peer(k))
            copies.append(
                remote(klbuf.at[stage], buf.at[place(k)], ss.at[k], rs.at[place(k)], peer(k))
            )

        def finish():
            value = klbuf[stage]
            for k in range(1, count):
                copies[k - 1].wait_recv()
                value = value + buf[place(k)]
            klbuf[stage + 1] = value

        return finish

    chunks((3, 5))
    chunks_wait((4,))
    a_step(0, 0)
    chunks_wait((3, 5))
    a_step(1, 1)
    bx_send((4, 3, 5))
    chunks((2, 6))
    a_step(1, 0)
    chunks_wait((2, 6))
    bx_send((2, 6))
    chunks((1, 7, 0))
    a_step(2, 1)
    chunks_wait((1, 7, 0))
    bx_send((1, 7, 0))
    remote(gb_part(p_partner, y), gb_part(p_partner, y), gb_s.at[0], gb_r.at[y], partner).wait_recv()
    for k in range(1, 4):
        send(
            gb_part(p_partner, y), gb_part(p_partner, y), gb_s.at[k], gb_r.at[y],
            dev(y_=(y + k) % 4),
        )
    send(gb_all(me4), gb_all(me4), gb_s.at[4], gb_r.at[4], sibling)
    others = (sibling, partner, partner_sibling)
    for n in range(3):
        send(gvs, gv.at[me4], gv_s.at[n], gv_r.at[n], others[n])
    gram_g(0, 2)
    a_step(2, 0)
    gram_g(2, 4)
    a_step(3, 1)
    gram_g(4, 6)
    a_step(3, 0)
    bx_wait((4, 3, 5))
    b_step(0, 0)
    b_step(1, 1)
    gram_g(6, 8)
    gram_a()

    for half in (0, 1):
        ring_last(half, arecv, a_s, a_r, a_sizes)

    def a_srcs(half):
        at = pl.multiple_of(half * CH, CH)
        return [
            load(own.at[z], at), load(crecv.at[z], at),
            load(arecv.at[0, half, 3]), load(arecv.at[1, half, 3]),
        ]

    add_rows(CH, store(xsend), a_srcs(1 - xh))
    send(xsend, xrecv, x_s.at[0], x_r.at[0], partner)
    add_rows(CH, store(xown), a_srcs(xh))
    b_step(1, 0)
    gram_core(0)
    gram_core(1)
    bx_wait((2, 6))
    b_step(2, 1)
    remote(xsend, xrecv, x_s.at[0], x_r.at[0], partner).wait_recv()
    add_rows(CH, store(eg.at[0, z]), [load(xown), load(xrecv)])
    gather(0, 0)
    b_step(2, 0)
    gram_x()
    bx_wait((1, 7, 0))
    b_step(3, 1)
    for k in range(1, 4):
        there = gb_part(p_partner, (y + k) % 4)
        remote(there, there, gb_s.at[k], gb_r.at[(y + k) % 4], dev(y_=(y + k) % 4)).wait_recv()
    send(gb_all(p_partner), gb_all(p_partner), gb_s.at[5], gb_r.at[5], sibling)
    gather(0, 1)
    b_step(3, 0)
    loc_ab = jnp.broadcast_to(avals[...].reshape(1, 2 * CC), (128, 2 * CC)).T
    ab[...] = loc_ab
    remote(gb_all(me4), gb_all(me4), gb_s.at[4], gb_r.at[4], sibling).wait_recv()
    remote(gb_all(p_partner), gb_all(p_partner), gb_s.at[5], gb_r.at[5], sibling).wait_recv()
    project(0, 0)
    gather(0, 2)
    project(0, 1)
    project(0, 7)
    for half in (0, 1):
        srcs = ring_last(half, brecv, b_s, b_r, part_sizes) + list(b_own(z, half))
        add_rows(PART, store(eg.at[1, z, pl.ds(half * PART, PART)]), srcs)
    gather(1, 0)
    gather(0, 3)
    project(0, 2)
    project(0, 6)
    project(1, 0)
    for i in range(NZ):
        for h in range(2):
            to = i * OB + h * HALF
            at = h * (OUT_WIN // 2) + i * HALF
            g4p[:, to : to + HALF] = g4[:, at : at + HALF]
    gather(1, 1)
    for n in range(3):
        remote(gvs, gv.at[me4], gv_s.at[n], gv_r.at[n], others[n]).wait_recv()
    gv[me4] = gvs[...]
    gather_last(0)
    kl_a = scale(0)
    back_chunks(0, (4,))
    back_step(0, 0, 0)
    back_chunks(0, (3, 5))
    back_step(0, 1, 1)
    gather(1, 2)
    project(1, 1)
    project(1, 7)
    back_chunks(0, (2, 6))
    gram_own()
    gather(1, 3)
    project(1, 2)
    project(1, 6)
    back_step(0, 1, 0)
    back_step(0, 2, 1)
    gather_last(1)
    kl_b = scale(1)
    klbuf[0] = jnp.full((8, 128), jnp.sum(kl_a + kl_b), F32)
    kl_z = kl_round(
        0, NZ, lambda k: (z + k) % NZ, lambda k: dev(z_=(z + k) % NZ), klz, klz_s, klz_r
    )
    back_chunks(1, (4,))
    back_step(1, 0, 0)
    back_chunks(1, (3, 5))
    back_step(1, 1, 1)
    gram_step(0, 0)
    gram_step(1, 1)
    back_chunks(0, (1, 7, 0))
    back_step(0, 2, 0)
    back_step(0, 3, 1)
    back_chunks(1, (2, 6))
    kl_z()
    kl_y = kl_round(
        1, 4, lambda k: (y + k) % 4, lambda k: dev(y_=(y + k) % 4), kly, kly_s, kly_r
    )
    back_step(1, 1, 0)
    back_step(1, 2, 1)
    gram_step(1, 0)
    back_step(0, 3, 0)
    gram_step(2, 1)
    back_chunks(1, (1, 7, 0))
    kl_y()
    kl_x = kl_round(
        2, 4,
        lambda k: (xh ^ (k // 2)) * 2 + (xl ^ (k % 2)),
        lambda k: dev(xh_=xh ^ (k // 2), xl_=xl ^ (k % 2)),
        klx, klx_s, klx_r,
    )
    back_step(1, 2, 0)
    back_step(1, 3, 1)
    gram_step(2, 0)
    final_send(0)
    back_step(1, 3, 0)
    gram_step(3, 1)
    kl_x()
    kl_c = kl_round(
        3, 2, lambda k: core if k == 0 else 1 - core, lambda k: sibling, klc, klc_s, klc_r
    )
    gram_step(3, 0)
    drain()
    final_send(1)
    out_a = final_dot(0)
    total[...] = out_a
    for half in (0, 1):
        srcs = ring_last(half, grecv, gz_s, gz_r, gram_sizes)
        srcs.append(load(gown.at[z], half * GL))
        size = gram_sizes[half]
        add_rows(size, store(gram.at[pl.ds(half * GL, size)]), srcs)
    kl_c()
    gain[...] = jnp.sqrt(OUT_WIN * FEAT / klbuf[4])
    total[...] = total[...] + final_dot(1)
    drain()


def finish(total, gram, gain, afac, gfac, update, new_a, new_g):
    update[...] = total[...] * gain[0:1, 0:1]
    fresh = (1.0 - DECAY) / TOKENS
    new_g[...] = DECAY * gfac[...] + fresh * gram[0:GW, :]
    new_a[:, 0:384] = DECAY * afac[:, 0:384] + fresh * gram[GW : GW + AW, :]
    new_a[:, 384:768] = DECAY * afac[:, 384:768] + fresh * gram[GW + AW : GR, :]


def per_device(
    activations, out_grads, a_basis, a_values, g_basis, g_values, owners, a_factors, g_factors
):
    workers = jnp.arange(owners.shape[1], dtype=jnp.int32)
    inverse = jnp.sum(
        jnp.where(owners[:, None, :] == workers[None, :, None], workers[None, None, :], 0), axis=2
    )
    vmem = pl.BlockSpec(memory_space=pltpu.VMEM)
    smem = pl.BlockSpec(memory_space=pltpu.SMEM)
    hbm = pl.BlockSpec(memory_space=pl.ANY)
    sem = pltpu.SemaphoreType.DMA
    v = pltpu.VMEM
    ring_a = (2, 2, 4, CH, OB)
    ring_b = (2, 2, 4, CH // 2, OB)
    scratch = [
        v((512, 768), BF16), v((512, OUT_WIN), BF16), v((768, 768), BF16),
        v((768, 768), BF16), v((768, 512), BF16), v((NZ, CC, OB), F32),
        v((NZ, CC, OB), BF16), v((NZ, CC, OB), BF16),
        v(ring_a, BF16), v(ring_a, BF16),
        v((CH, OB), BF16), v((CH, OB), BF16), v((CH, OB), F32),
        v((NZ, CH, OB), BF16), v((NZ, CH, OB), BF16), v(ring_b, BF16), v(ring_b, BF16),
        v((2, NZ, CH, OB), BF16), v((4 * GW, OUT_WIN), BF16), v((4 * GW, OUT_WIN), BF16),
        v((4, 8, GW), F32), v((8, GW), F32),
        v((768, 128), F32), v((2, CH, OB), F32), v((2, CH, OB), BF16),
        v((2, NZ, CH, OB), F32), v((2, *ring_b), BF16), v((2, *ring_b), BF16),
        v((2, 4, GW, CH), BF16), v((2, 4, GW, CH), BF16),
        v((32, GW, OB), F32), v((32, AW, 768), F32),
        v((2, NZ, GR, OB), BF16), v((2, NZ, GR, OB), BF16),
        v((NZ, GR, OB), BF16), v((NZ, GR, OB), BF16), v((NZ, GR, OB), F32),
        v((2, 2, 4, GL, OB), BF16), v((2, 2, 4, GL, OB), BF16),
        v((5, 8, 128), F32), v((NZ, 8, 128), F32), v((4, 8, 128), F32), v((4, 8, 128), F32),
        v((2, 8, 128), F32),
        sem((NZ,)), sem((NZ,)), sem((2, 2, 4)), sem((2, 2, 4)), sem((1,)), sem((1,)),
        sem((NZ,)), sem((NZ,)), sem((2, 2, 4)), sem((2, 2, 4)),
        sem((2, 2, 2, 4)), sem((2, 2, 2, 4)), sem((2, 2, 2, 4)), sem((2, 2, 2, 4)),
        sem((2, 3)), sem((2, 3)),
        sem((2,)), sem((2,)), sem((1,)), sem((1,)), sem((2, 2, 4)), sem((2, 2, 4)),
        sem((6,)), sem((6,)), sem((3,)), sem((3,)),
        sem((NZ,)), sem((NZ,)), sem((4,)), sem((4,)), sem((4,)), sem((4,)), sem((2,)), sem((2,)),
        sem((6,)),
    ]
    total, gram, gain = pl.pallas_call(
        kernel,
        out_shape=(
            jax.ShapeDtypeStruct((GW, 768), F32),
            jax.ShapeDtypeStruct((GR, OB), F32),
            jax.ShapeDtypeStruct((8, 128), F32),
        ),
        in_specs=[hbm] * 4 + [vmem] * 2 + [smem],
        out_specs=(vmem, vmem, vmem),
        scratch_shapes=scratch,
        compiler_params=pltpu.CompilerParams(
            collective_id=0, has_side_effects=True, vmem_limit_bytes=60 << 20
        ),
        cost_estimate=pl.CostEstimate(
            flops=5_400_000_000, bytes_accessed=8_000_000, transcendentals=0
        ),
        name="precondition",
    )(activations, out_grads, a_basis, g_basis.T, a_values, g_values, inverse)
    return pl.pallas_call(
        finish,
        out_shape=(
            jax.ShapeDtypeStruct((GW, 768), F32),
            jax.ShapeDtypeStruct((AW, 768), F32),
            jax.ShapeDtypeStruct((GW, OB), F32),
        ),
        in_specs=[vmem] * 5,
        out_specs=(vmem, vmem, vmem),
        name="finish",
    )(total, gram, gain, a_factors, g_factors)


def solution(mesh):
    in_specs = (
        P("dp", "tensor"),
        P("dp", None),
        P("tensor", None),
        P("tensor"),
        P(None, "dp"),
        P("dp"),
        P(),
        P("dp", "tensor"),
        P("dp", "tensor"),
    )
    out_specs = (P("dp", "tensor"), P("dp", "tensor"), P("dp", "tensor"))
    return jax.shard_map(
        per_device, mesh=mesh, in_specs=in_specs, out_specs=out_specs, check_vma=False
    )
```

time: 109 us -> 88.2 us (0.81)
  Pallas kernels: 102 us -> 86.1 us
  local copies, waits for them, and re-layouts: 4.79 us -> 0 us
    pallas_call x1, Pallas kernels: 102 us -> 84.1 us  [per_device(): pl.pallas_call(kernel, out_shape=(jax.ShapeDtypeStruct((GW, 768), F32), j...]
    unnamed x3 -> x0, local copies, waits for them, and re-layouts: 4.79 us -> none
    pallas_call x0 -> x1, Pallas kernels: none -> 1.96 us  [per_device(): pl.pallas_call(finish, out_shape=(jax.ShapeDtypeStruct((GW, 768), F32), j...]
where the time goes in v2:
time: 88.2 us; the launch traced here: 88.1 us
  Pallas kernels  86.1 us (98%)
  other arithmetic  1.36 us (2%)
    pallas_call x1, Pallas kernels, per_device(): pl.pallas_call(kernel, out_shape=(jax.ShapeDtypeStruct((GW, 768), F32), j...  84.1 us
    pallas_call x1, Pallas kernels, per_device(): pl.pallas_call(finish, out_shape=(jax.ShapeDtypeStruct((GW, 768), F32), j...  1.96 us

profile of v2, /device:TPU:1, one launch (start us, length us, event | category | flops | bytes accessed | tf_op | source)
XLA Modules:
  0.0 88.1 jit_solution(17595720443644308195)
XLA Ops:
  0.6 1.4 %select_reduce_fusion.inv = s32[2,32]{1,0:T(2,128)} fusion(s32[2,32]{1,0:T(2,128)} %param.15), kind=kLoop, calls=%fused_computation | loop fusion | flops 6080 | bytes 512 | tf_op jit(solution)/shard_map/reduce_sum | solution.py:618
  2.0 84.1 %precondition.1 = (f32[96,768]{1,0:T(8,128)}, f32[144,384]{1,0:T(8,128)}, f32[8,128]{1,0:T(8,128)}) custom-call(bf16[512,768]{1,0:T(8,128)(2,1)} %acts_in.1, bf16[512,3072]{1,0:T(8,128)(2,1)} %grads_in.1, bf16[768,768]{1,0:T(8,128)(2,1)} %qa_in.1, bf16[96,3072]{1,0:T(8,128)(2,1)} %bitcast.1, f32[768]{0:T(1024)} %avals.1, f32[96]{0:T(128)} %gvals.1, ...), custom_call_target="tpu_custom_call" | custom-call | flops 5400000000 | bytes 8000000 | tf_op jit(solution)/shard_map/precondition/pallas_call | solution.py:655
  86.1 2.0 %finish.1 = (f32[96,768]{1,0:T(8,128)}, f32[24,768]{1,0:T(8,128)}, f32[96,384]{1,0:T(8,128)}) custom-call(f32[96,768]{1,0:T(8,128)} %get-tuple-element.6.total, f32[144,384]{1,0:T(8,128)} %get-tuple-element.7.gram, f32[8,128]{1,0:T(8,128)} %get-tuple-element.8.gain, f32[24,768]{1,0:T(8,128)} %afac.1, f32[96,384]{1,0:T(8,128)} %gfac.1), custom_call_target="tpu_custom_call" | custom-call | tf_op jit(solution)/shard_map/finish/pallas_call | solution.py:673

commit v3 on v2

--- a/solution.py
+++ b/solution.py
@@ -61,14 +61,14 @@
 
 
 def kernel(
-    acts_in, grads_in, qa_in, gbasis_in, avals, gvals, inv,
+    acts_in, grads_in, qa_in, gbasis_in, avals, gvals, owners,
     total, gram, gain,
     acts, grads, qa, qat, apt, own, csend, crecv,
     asend, arecv, xsend, xrecv, xown, xbs, xbr, bsend, brecv,
     eg, g4, g4p, gv, gvs, ab, proj, scl,
     rown, rsend, rrecv, fsend, frecv,
     gramg, grama, gcs, gcr, gxs, gxr, gown, gsend, grecv,
-    klbuf, klz, kly, klx, klc,
+    klbuf, klz, kly, klx, klc, inv_rows, inv,
     c_s, c_r, a_s, a_r, x_s, x_r, xb_s, xb_r, b_s, b_r, e_s, e_r, r_s, r_r, f_s, f_r,
     gc_s, gc_r, gx_s, gx_r, gz_s, gz_r, gb_s, gb_r, gv_s, gv_r,
     klz_s, klz_r, kly_s, kly_r, klx_s, klx_r, klc_s, klc_r, loc,
@@ -101,10 +101,11 @@
         pending.append(copy)
         return copy
 
-    def drain():
-        for copy in pending:
+    def drain(keep=0):
+        old = pending[: len(pending) - keep]
+        for copy in old:
             copy.wait_send()
-        pending.clear()
+        del pending[: len(old)]
 
     barrier = pltpu.get_barrier_semaphore()
 
@@ -131,6 +132,14 @@
     greet(dev(xl_=1 - xl))
     greet(dev(xh_=1 - xh, xl_=1 - xl))
 
+    for i in range(2):
+        worker = lax.broadcasted_iota(jnp.int32, (32, 32), 0)
+        block = lax.broadcasted_iota(jnp.int32, (32, 32), 1)
+        here = jnp.where(jnp.broadcast_to(owners[i : i + 1, :], (32, 32)) == worker, block, 0)
+        inv_rows[i] = jnp.broadcast_to(jnp.max(here, axis=1, keepdims=True), (32, 128))
+    inv_copy = pltpu.make_async_copy(inv_rows, inv, loc.at[6])
+    inv_copy.start()
+
     loads[0].wait()
     for i in range(6):
         qat[128 * i : 128 * (i + 1), :] = qa[:, 128 * i : 128 * (i + 1)].T
@@ -275,7 +284,7 @@
 
     def gram_block(xh_, z_, core_):
         w = (xh_ * NZ + z_) * 2 + core_
-        return gramg[inv[1, w]], grama[inv[0, w]]
+        return gramg[inv[1, w, 0]], grama[inv[0, w, 0]]
 
     def put_block(ref, g_part, a_part):
         ref[0:GW, :] = g_part.astype(ref.dtype)
@@ -292,23 +301,29 @@
         lax.fori_loop(0, NZ, body, 0)
         send(gcs.at[turn], gcr.at[turn], gc_s.at[turn], gc_r.at[turn], sibling)
 
-    def gram_sum(dst, xh_, others):
-        def body(i, _):
-            put_block(gown.at[i], *gram_block(xh_, i, core))
-            add_rows(GR, store(dst.at[i]), [load(gown.at[i])] + [load(o.at[i]) for o in others])
-            return 0
-
-        lax.fori_loop(0, NZ, body, 0)
-
-    def gram_x():
-        remote(gcs.at[0], gcr.at[0], gc_s.at[0], gc_r.at[0], sibling).wait_recv()
-        gram_sum(gxs, 1 - xh, [gcr.at[0]])
-        send(gxs, gxr, gx_s.at[0], gx_r.at[0], partner)
-
-    def gram_own():
-        remote(gcs.at[1], gcr.at[1], gc_s.at[1], gc_r.at[1], sibling).wait_recv()
-        remote(gxs, gxr, gx_s.at[0], gx_r.at[0], partner).wait_recv()
-        gram_sum(gown, xh, [gcr.at[1], gxr])
+    def gram_add(d, dst, xh_, others):
+        put_block(gown.at[d], *gram_block(xh_, d, core))
+        add_rows(GR, store(dst), [load(gown.at[d])] + [load(other) for other in others])
+
+    def gx_copy(d):
+        return remote(gxs.at[d], gxr.at[d], gx_s.at[d], gx_r.at[d], partner)
+
+    def gram_wait(turn):
+        remote(gcs.at[turn], gcr.at[turn], gc_s.at[turn], gc_r.at[turn], sibling).wait_recv()
+
+    def gram_x(ks):
+        for k in ks:
+            d = (z + k) % NZ
+            gram_add(d, gxs.at[d], 1 - xh, [gcr.at[0, d]])
+            copy = gx_copy(d)
+            copy.start()
+            pending.append(copy)
+
+    def gram_own(ks):
+        for k in ks:
+            d = (z + k) % NZ
+            gx_copy(d).wait_recv()
+            gram_add(d, gown.at[d], xh, [gcr.at[1, d], gxr.at[d]])
 
     def gram_half(d, half):
         return (load(gown.at[d], half * GL),)
@@ -436,114 +451,149 @@
 
         return finish
 
+    def gb_forward():
+        part = gb_part(p_partner, y)
+        remote(part, part, gb_s.at[0], gb_r.at[y], partner).wait_recv()
+        for k in range(1, 4):
+            send(part, part, gb_s.at[k], gb_r.at[y], dev(y_=(y + k) % 4))
+        send(gb_all(me4), gb_all(me4), gb_s.at[4], gb_r.at[4], sibling)
+
+    def gb_sibling():
+        for k in range(1, 4):
+            y_ = (y + k) % 4
+            there = gb_part(p_partner, y_)
+            remote(there, there, gb_s.at[k], gb_r.at[y_], dev(y_=y_)).wait_recv()
+        send(gb_all(p_partner), gb_all(p_partner), gb_s.at[5], gb_r.at[5], sibling)
+
+    def gb_wait():
+        for n, p in ((4, me4), (5, p_partner)):
+            remote(gb_all(p), gb_all(p), gb_s.at[n], gb_r.at[n], sibling).wait_recv()
+
+    others = (sibling, partner, partner_sibling)
+
+    def gv_copy(n):
+        return remote(gvs, gv.at[me4], gv_s.at[n], gv_r.at[n], others[n])
+
+    def turn_columns():
+        for i in range(NZ):
+            for h in range(2):
+                to = i * OB + h * HALF
+                at = h * (OUT_WIN // 2) + i * HALF
+                g4p[:, to : to + HALF] = g4[:, at : at + HALF]
+
+    def a_last():
+        for half in (0, 1):
+            ring_last(half, arecv, a_s, a_r, a_sizes)
+
+        def srcs(half):
+            at = pl.multiple_of(half * CH, CH)
+            return [
+                load(own.at[z], at), load(crecv.at[z], at),
+                load(arecv.at[0, half, 3]), load(arecv.at[1, half, 3]),
+            ]
+
+        add_rows(CH, store(xsend), srcs(1 - xh))
+        send(xsend, xrecv, x_s.at[0], x_r.at[0], partner)
+        add_rows(CH, store(xown), srcs(xh))
+
+    def a_done():
+        remote(xsend, xrecv, x_s.at[0], x_r.at[0], partner).wait_recv()
+        add_rows(CH, store(eg.at[0, z]), [load(xown), load(xrecv)])
+
+    def b_done():
+        for half in (0, 1):
+            srcs = ring_last(half, brecv, b_s, b_r, part_sizes) + list(b_own(z, half))
+            add_rows(PART, store(eg.at[1, z, pl.ds(half * PART, PART)]), srcs)
+
     chunks((3, 5))
     chunks_wait((4,))
     a_step(0, 0)
+    bx_send((4,))
     chunks_wait((3, 5))
     a_step(1, 1)
-    bx_send((4, 3, 5))
+    bx_send((3, 5))
     chunks((2, 6))
+    gram_g(0, 2)
     a_step(1, 0)
     chunks_wait((2, 6))
     bx_send((2, 6))
     chunks((1, 7, 0))
     a_step(2, 1)
+    bx_wait((4,))
+    b_step(0, 0)
     chunks_wait((1, 7, 0))
     bx_send((1, 7, 0))
-    remote(gb_part(p_partner, y), gb_part(p_partner, y), gb_s.at[0], gb_r.at[y], partner).wait_recv()
-    for k in range(1, 4):
-        send(
-            gb_part(p_partner, y), gb_part(p_partner, y), gb_s.at[k], gb_r.at[y],
-            dev(y_=(y + k) % 4),
-        )
-    send(gb_all(me4), gb_all(me4), gb_s.at[4], gb_r.at[4], sibling)
-    others = (sibling, partner, partner_sibling)
+    gram_g(2, 3)
+    a_step(2, 0)
+    gb_forward()
     for n in range(3):
-        send(gvs, gv.at[me4], gv_s.at[n], gv_r.at[n], others[n])
-    gram_g(0, 2)
-    a_step(2, 0)
-    gram_g(2, 4)
+        copy = gv_copy(n)
+        copy.start()
+        pending.append(copy)
+    bx_wait((3, 5))
+    b_step(1, 1)
+    gram_g(3, 4)
     a_step(3, 1)
+    b_step(1, 0)
     gram_g(4, 6)
     a_step(3, 0)
-    bx_wait((4, 3, 5))
-    b_step(0, 0)
-    b_step(1, 1)
-    gram_g(6, 8)
-    gram_a()
-
-    for half in (0, 1):
-        ring_last(half, arecv, a_s, a_r, a_sizes)
-
-    def a_srcs(half):
-        at = pl.multiple_of(half * CH, CH)
-        return [
-            load(own.at[z], at), load(crecv.at[z], at),
-            load(arecv.at[0, half, 3]), load(arecv.at[1, half, 3]),
-        ]
-
-    add_rows(CH, store(xsend), a_srcs(1 - xh))
-    send(xsend, xrecv, x_s.at[0], x_r.at[0], partner)
-    add_rows(CH, store(xown), a_srcs(xh))
-    b_step(1, 0)
-    gram_core(0)
-    gram_core(1)
     bx_wait((2, 6))
     b_step(2, 1)
-    remote(xsend, xrecv, x_s.at[0], x_r.at[0], partner).wait_recv()
-    add_rows(CH, store(eg.at[0, z]), [load(xown), load(xrecv)])
+    gram_g(6, 8)
+    b_step(2, 0)
+    gram_a()
+    a_last()
+    inv_copy.wait()
+    gram_core(0)
+    bx_wait((1, 7))
+    b_step(3, 1)
+    gram_core(1)
+    b_step(3, 0)
+    gram_wait(0)
+    gram_x((4, 3, 5))
+    a_done()
     gather(0, 0)
-    b_step(2, 0)
-    gram_x()
-    bx_wait((1, 7, 0))
-    b_step(3, 1)
-    for k in range(1, 4):
-        there = gb_part(p_partner, (y + k) % 4)
-        remote(there, there, gb_s.at[k], gb_r.at[(y + k) % 4], dev(y_=(y + k) % 4)).wait_recv()
-    send(gb_all(p_partner), gb_all(p_partner), gb_s.at[5], gb_r.at[5], sibling)
+    bx_wait((0,))
+    b_done()
+    gather(1, 0)
+    gram_x((2, 6, 1, 7, 0))
+    gram_wait(1)
+    gb_sibling()
+    ab[...] = jnp.broadcast_to(avals[...].reshape(1, 2 * CC), (128, 2 * CC)).T
     gather(0, 1)
-    b_step(3, 0)
-    loc_ab = jnp.broadcast_to(avals[...].reshape(1, 2 * CC), (128, 2 * CC)).T
-    ab[...] = loc_ab
-    remote(gb_all(me4), gb_all(me4), gb_s.at[4], gb_r.at[4], sibling).wait_recv()
-    remote(gb_all(p_partner), gb_all(p_partner), gb_s.at[5], gb_r.at[5], sibling).wait_recv()
+    gram_own((4,))
+    gram_step(0, 0)
+    gather(1, 1)
+    gb_wait()
     project(0, 0)
+    project(1, 0)
+    gram_own((3, 5))
+    gram_step(1, 1)
+    for k in (1, 7):
+        project(0, k)
     gather(0, 2)
-    project(0, 1)
-    project(0, 7)
-    for half in (0, 1):
-        srcs = ring_last(half, brecv, b_s, b_r, part_sizes) + list(b_own(z, half))
-        add_rows(PART, store(eg.at[1, z, pl.ds(half * PART, PART)]), srcs)
-    gather(1, 0)
+    for k in (1, 7):
+        project(1, k)
+    gather(1, 2)
+    gram_step(1, 0)
+    turn_columns()
+    for n in range(3):
+        gv_copy(n).wait_recv()
+    gv[me4] = gvs[...]
+    for k in (2, 6):
+        project(0, k)
     gather(0, 3)
-    project(0, 2)
-    project(0, 6)
-    project(1, 0)
-    for i in range(NZ):
-        for h in range(2):
-            to = i * OB + h * HALF
-            at = h * (OUT_WIN // 2) + i * HALF
-            g4p[:, to : to + HALF] = g4[:, at : at + HALF]
-    gather(1, 1)
-    for n in range(3):
-        remote(gvs, gv.at[me4], gv_s.at[n], gv_r.at[n], others[n]).wait_recv()
-    gv[me4] = gvs[...]
+    gram_own((2, 6))
+    gram_step(2, 1)
+    for k in (2, 6):
+        project(1, k)
+    gather(1, 3)
     gather_last(0)
     kl_a = scale(0)
     back_chunks(0, (4,))
     back_step(0, 0, 0)
     back_chunks(0, (3, 5))
     back_step(0, 1, 1)
-    gather(1, 2)
-    project(1, 1)
-    project(1, 7)
-    back_chunks(0, (2, 6))
-    gram_own()
-    gather(1, 3)
-    project(1, 2)
-    project(1, 6)
-    back_step(0, 1, 0)
-    back_step(0, 2, 1)
     gather_last(1)
     kl_b = scale(1)
     klbuf[0] = jnp.full((8, 128), jnp.sum(kl_a + kl_b), F32)
@@ -554,22 +604,25 @@
     back_step(1, 0, 0)
     back_chunks(1, (3, 5))
     back_step(1, 1, 1)
-    gram_step(0, 0)
-    gram_step(1, 1)
-    back_chunks(0, (1, 7, 0))
-    back_step(0, 2, 0)
-    back_step(0, 3, 1)
+    back_chunks(0, (2, 6))
+    back_step(0, 1, 0)
+    back_step(0, 2, 1)
     back_chunks(1, (2, 6))
+    back_step(1, 1, 0)
+    back_step(1, 2, 1)
+    gram_step(2, 0)
+    gram_own((1, 7, 0))
     kl_z()
     kl_y = kl_round(
         1, 4, lambda k: (y + k) % 4, lambda k: dev(y_=(y + k) % 4), kly, kly_s, kly_r
     )
-    back_step(1, 1, 0)
-    back_step(1, 2, 1)
-    gram_step(1, 0)
-    back_step(0, 3, 0)
-    gram_step(2, 1)
+    back_chunks(0, (1, 7, 0))
+    back_step(0, 2, 0)
+    back_step(0, 3, 1)
     back_chunks(1, (1, 7, 0))
+    back_step(1, 2, 0)
+    back_step(1, 3, 1)
+    gram_step(3, 1)
     kl_y()
     kl_x = kl_round(
         2, 4,
@@ -577,28 +630,26 @@
         lambda k: dev(xh_=xh ^ (k // 2), xl_=xl ^ (k % 2)),
         klx, klx_s, klx_r,
     )
-    back_step(1, 2, 0)
-    back_step(1, 3, 1)
-    gram_step(2, 0)
-    final_send(0)
+    drain(24)
+    back_step(0, 3, 0)
     back_step(1, 3, 0)
-    gram_step(3, 1)
+    gram_step(3, 0)
     kl_x()
     kl_c = kl_round(
         3, 2, lambda k: core if k == 0 else 1 - core, lambda k: sibling, klc, klc_s, klc_r
     )
-    gram_step(3, 0)
-    drain()
+    final_send(0)
     final_send(1)
     out_a = final_dot(0)
     total[...] = out_a
+    kl_c()
+    gain[...] = jnp.sqrt(OUT_WIN * FEAT / klbuf[4])
+    drain(12)
     for half in (0, 1):
         srcs = ring_last(half, grecv, gz_s, gz_r, gram_sizes)
         srcs.append(load(gown.at[z], half * GL))
         size = gram_sizes[half]
         add_rows(size, store(gram.at[pl.ds(half * GL, size)]), srcs)
-    kl_c()
-    gain[...] = jnp.sqrt(OUT_WIN * FEAT / klbuf[4])
     total[...] = total[...] + final_dot(1)
     drain()
 
@@ -614,12 +665,7 @@
 def per_device(
     activations, out_grads, a_basis, a_values, g_basis, g_values, owners, a_factors, g_factors
 ):
-    workers = jnp.arange(owners.shape[1], dtype=jnp.int32)
-    inverse = jnp.sum(
-        jnp.where(owners[:, None, :] == workers[None, :, None], workers[None, None, :], 0), axis=2
-    )
     vmem = pl.BlockSpec(memory_space=pltpu.VMEM)
-    smem = pl.BlockSpec(memory_space=pltpu.SMEM)
     hbm = pl.BlockSpec(memory_space=pl.ANY)
     sem = pltpu.SemaphoreType.DMA
     v = pltpu.VMEM
@@ -642,15 +688,15 @@
         v((NZ, GR, OB), BF16), v((NZ, GR, OB), BF16), v((NZ, GR, OB), F32),
         v((2, 2, 4, GL, OB), BF16), v((2, 2, 4, GL, OB), BF16),
         v((5, 8, 128), F32), v((NZ, 8, 128), F32), v((4, 8, 128), F32), v((4, 8, 128), F32),
-        v((2, 8, 128), F32),
+        v((2, 8, 128), F32), v((2, 32, 128), jnp.int32), pltpu.SMEM((2, 32, 128), jnp.int32),
         sem((NZ,)), sem((NZ,)), sem((2, 2, 4)), sem((2, 2, 4)), sem((1,)), sem((1,)),
         sem((NZ,)), sem((NZ,)), sem((2, 2, 4)), sem((2, 2, 4)),
         sem((2, 2, 2, 4)), sem((2, 2, 2, 4)), sem((2, 2, 2, 4)), sem((2, 2, 2, 4)),
         sem((2, 3)), sem((2, 3)),
-        sem((2,)), sem((2,)), sem((1,)), sem((1,)), sem((2, 2, 4)), sem((2, 2, 4)),
+        sem((2,)), sem((2,)), sem((NZ,)), sem((NZ,)), sem((2, 2, 4)), sem((2, 2, 4)),
         sem((6,)), sem((6,)), sem((3,)), sem((3,)),
         sem((NZ,)), sem((NZ,)), sem((4,)), sem((4,)), sem((4,)), sem((4,)), sem((2,)), sem((2,)),
-        sem((6,)),
+        sem((7,)),
     ]
     total, gram, gain = pl.pallas_call(
         kernel,
@@ -659,7 +705,7 @@
             jax.ShapeDtypeStruct((GR, OB), F32),
             jax.ShapeDtypeStruct((8, 128), F32),
         ),
-        in_specs=[hbm] * 4 + [vmem] * 2 + [smem],
+        in_specs=[hbm] * 4 + [vmem] * 3,
         out_specs=(vmem, vmem, vmem),
         scratch_shapes=scratch,
         compiler_params=pltpu.CompilerParams(
@@ -669,7 +715,7 @@
             flops=5_400_000_000, bytes_accessed=8_000_000, transcendentals=0
         ),
         name="precondition",
-    )(activations, out_grads, a_basis, g_basis.T, a_values, g_values, inverse)
+    )(activations, out_grads, a_basis, g_basis.T, a_values, g_values, owners)
     return pl.pallas_call(
         finish,
         out_shape=(

time: 88.2 us -> 80.3 us (0.910)
  Pallas kernels: 86.1 us -> 79.5 us
  other arithmetic: 1.36 us -> 0 us
    pallas_call x1, Pallas kernels: 84.1 us -> 77.5 us  [per_device(): pl.pallas_call(kernel, out_shape=(jax.ShapeDtypeStruct((GW, 768), F32), j...]
    reduce_sum x1 -> x0, other arithmetic: 1.36 us -> none  [per_device(): jnp.sum(jnp.where(owners[:, None, :] == workers[None, :, None], workers[N...]
where the time goes in v3:
time: 80.3 us; the launch traced here: 80.1 us
  Pallas kernels  79.5 us (99%)
    pallas_call x1, Pallas kernels, per_device(): pl.pallas_call(kernel, out_shape=(jax.ShapeDtypeStruct((GW, 768), F32), j...  77.5 us
    pallas_call x1, Pallas kernels, per_device(): pl.pallas_call(finish, out_shape=(jax.ShapeDtypeStruct((GW, 768), F32), j...  1.96 us

profile of v3, /device:TPU:1, one launch (start us, length us, event | category | flops | bytes accessed | tf_op | source)
XLA Modules:
  0.0 80.1 jit_solution(7357818506773250722)
XLA Ops:
  0.6 77.5 %precondition.1 = (f32[96,768]{1,0:T(8,128)}, f32[144,384]{1,0:T(8,128)}, f32[8,128]{1,0:T(8,128)}) custom-call(bf16[512,768]{1,0:T(8,128)(2,1)} %acts_in.1, bf16[512,3072]{1,0:T(8,128)(2,1)} %grads_in.1, bf16[768,768]{1,0:T(8,128)(2,1)} %qa_in.1, bf16[96,3072]{1,0:T(8,128)(2,1)} %bitcast.1, f32[768]{0:T(1024)} %avals.1, f32[96]{0:T(128)} %gvals.1, ...), custom_call_target="tpu_custom_call" | custom-call | flops 5400000000 | bytes 8000000 | tf_op jit(solution)/shard_map/precondition/pallas_call | solution.py:701
  78.2 2.0 %finish.1 = (f32[96,768]{1,0:T(8,128)}, f32[24,768]{1,0:T(8,128)}, f32[96,384]{1,0:T(8,128)}) custom-call(f32[96,768]{1,0:T(8,128)} %get-tuple-element.6.total, f32[144,384]{1,0:T(8,128)} %get-tuple-element.7.gram, f32[8,128]{1,0:T(8,128)} %get-tuple-element.8.gain, f32[24,768]{1,0:T(8,128)} %afac.1, f32[96,384]{1,0:T(8,128)} %gfac.1), custom_call_target="tpu_custom_call" | custom-call | tf_op jit(solution)/shard_map/finish/pallas_call | solution.py:719

commit v4 on v3

--- a/solution.py
+++ b/solution.py
@@ -34,7 +34,9 @@
     return lax.dot_general(a, b, dims, preferred_element_type=F32)
 
 
-def add_rows(rows, dst, srcs, step=16):
+def add_rows(rows, dst, srcs):
+    step = 48 if rows % 48 == 0 else 16
+
     def body(i, _):
         at = pl.ds(pl.multiple_of(i * step, step), step)
         total = srcs[0](at).astype(F32)
@@ -43,7 +45,7 @@
         dst(at, total)
         return 0
 
-    lax.fori_loop(0, rows // step, body, 0, unroll=2)
+    lax.fori_loop(0, rows // step, body, 0, unroll=rows // step)
 
 
 def store(ref):
@@ -125,8 +127,8 @@
     greet(sibling)
     greet(partner)
     greet(partner_sibling)
-    for k in range(1, NZ):
-        greet(dev(z_=(z + k) % NZ))
+    greet(ring[0])
+    greet(ring[1])
     for k in range(1, 4):
         greet(dev(y_=(y + k) % 4))
     greet(dev(xl_=1 - xl))
@@ -167,7 +169,7 @@
     d0, block0 = chunk(4)
     loads[3].wait()
     gvs[...] = jnp.broadcast_to(gvals[...].reshape(1, GW), gvs.shape)
-    pl.semaphore_wait(barrier, 15)
+    pl.semaphore_wait(barrier, 10)
     pending.append(chunk_send(d0))
     pending[-1].start()
 
@@ -181,7 +183,6 @@
         return g4.at[pl.ds(pl.multiple_of(p * GW, GW), GW)]
 
     p_partner = (1 - xh) * 2 + core
-    send(gb_part(me4, y), gb_part(me4, y), gb_s.at[0], gb_r.at[y], partner)
     chunk_own(d0, block0)
 
     def offset(direction, it):
@@ -512,6 +513,7 @@
     chunks_wait((3, 5))
     a_step(1, 1)
     bx_send((3, 5))
+    send(gb_part(me4, y), gb_part(me4, y), gb_s.at[0], gb_r.at[y], partner)
     chunks((2, 6))
     gram_g(0, 2)
     a_step(1, 0)
@@ -525,11 +527,6 @@
     bx_send((1, 7, 0))
     gram_g(2, 3)
     a_step(2, 0)
-    gb_forward()
-    for n in range(3):
-        copy = gv_copy(n)
-        copy.start()
-        pending.append(copy)
     bx_wait((3, 5))
     b_step(1, 1)
     gram_g(3, 4)
@@ -537,6 +534,11 @@
     b_step(1, 0)
     gram_g(4, 6)
     a_step(3, 0)
+    gb_forward()
+    for n in range(3):
+        copy = gv_copy(n)
+        copy.start()
+        pending.append(copy)
     bx_wait((2, 6))
     b_step(2, 1)
     gram_g(6, 8)
@@ -610,7 +612,6 @@
     back_chunks(1, (2, 6))
     back_step(1, 1, 0)
     back_step(1, 2, 1)
-    gram_step(2, 0)
     gram_own((1, 7, 0))
     kl_z()
     kl_y = kl_round(
@@ -622,7 +623,7 @@
     back_chunks(1, (1, 7, 0))
     back_step(1, 2, 0)
     back_step(1, 3, 1)
-    gram_step(3, 1)
+    gram_step(2, 0)
     kl_y()
     kl_x = kl_round(
         2, 4,
@@ -633,6 +634,7 @@
     drain(24)
     back_step(0, 3, 0)
     back_step(1, 3, 0)
+    gram_step(3, 1)
     gram_step(3, 0)
     kl_x()
     kl_c = kl_round(

time: 80.3 us -> 78.2 us (0.974)
  Pallas kernels: 79.5 us -> 77.5 us
    pallas_call x1, Pallas kernels: 77.5 us -> 75.5 us  [per_device(): pl.pallas_call(kernel, out_shape=(jax.ShapeDtypeStruct((GW, 768), F32), j...]
where the time goes in v4:
time: 78.2 us; the launch traced here: 78.1 us
  Pallas kernels  77.5 us (99%)
    pallas_call x1, Pallas kernels, per_device(): pl.pallas_call(kernel, out_shape=(jax.ShapeDtypeStruct((GW, 768), F32), j...  75.5 us
    pallas_call x1, Pallas kernels, per_device(): pl.pallas_call(finish, out_shape=(jax.ShapeDtypeStruct((GW, 768), F32), j...  1.96 us

profile of v4, /device:TPU:1, one launch (start us, length us, event | category | flops | bytes accessed | tf_op | source)
XLA Modules:
  0.0 78.1 jit_solution(5509246692343174414)
XLA Ops:
  0.6 75.5 %precondition.1 = (f32[96,768]{1,0:T(8,128)}, f32[144,384]{1,0:T(8,128)}, f32[8,128]{1,0:T(8,128)}) custom-call(bf16[512,768]{1,0:T(8,128)(2,1)} %acts_in.1, bf16[512,3072]{1,0:T(8,128)(2,1)} %grads_in.1, bf16[768,768]{1,0:T(8,128)(2,1)} %qa_in.1, bf16[96,3072]{1,0:T(8,128)(2,1)} %bitcast.1, f32[768]{0:T(1024)} %avals.1, f32[96]{0:T(128)} %gvals.1, ...), custom_call_target="tpu_custom_call" | custom-call | flops 5400000000 | bytes 8000000 | tf_op jit(solution)/shard_map/precondition/pallas_call | solution.py:703
  76.1 2.0 %finish.1 = (f32[96,768]{1,0:T(8,128)}, f32[24,768]{1,0:T(8,128)}, f32[96,384]{1,0:T(8,128)}) custom-call(f32[96,768]{1,0:T(8,128)} %get-tuple-element.6.total, f32[144,384]{1,0:T(8,128)} %get-tuple-element.7.gram, f32[8,128]{1,0:T(8,128)} %get-tuple-element.8.gain, f32[24,768]{1,0:T(8,128)} %afac.1, f32[96,384]{1,0:T(8,128)} %gfac.1), custom_call_target="tpu_custom_call" | custom-call | tf_op jit(solution)/shard_map/finish/pallas_call | solution.py:721

commit v5 on v4

--- a/solution.py
+++ b/solution.py
@@ -67,7 +67,7 @@
     total, gram, gain,
     acts, grads, qa, qat, apt, own, csend, crecv,
     asend, arecv, xsend, xrecv, xown, xbs, xbr, bsend, brecv,
-    eg, g4, g4p, gv, gvs, ab, proj, scl,
+    eg, g4, g4p, gv, gvs, ab, den, proj, scl,
     rown, rsend, rrecv, fsend, frecv,
     gramg, grama, gcs, gcr, gxs, gxr, gown, gsend, grecv,
     klbuf, klz, kly, klx, klc, inv_rows, inv,
@@ -366,19 +366,29 @@
         part = dot(eg[s, b], g4[:, pl.ds(pl.multiple_of(b * OB, 128), OB)], NT)
         proj[s] = part if k == 0 else proj[s] + part
 
-    def scale(s):
+    def denominators(s):
         g_row = jnp.concatenate([gv[p, 0:1, :] for p in range(4)], axis=1)
         first = core * CC + s * HALF + xh * CH
 
+        def body(i, _):
+            at = pl.multiple_of(i * 16, 16)
+            a_col = ab[pl.ds(pl.multiple_of(first + at, 16), 16), 0:1]
+            den[s, pl.ds(at, 16), :] = a_col * g_row + DAMPING
+            return 0
+
+        lax.fori_loop(0, CH // 16, body, 0)
+
+    def scale(s):
         def body(i, kl):
             at = pl.multiple_of(i * 16, 16)
             value = proj[s, pl.ds(at, 16), :]
-            a_col = ab[pl.ds(pl.multiple_of(first + at, 16), 16), 0:1]
-            scaled = value / (a_col * g_row + DAMPING)
+            scaled = value / den[s, pl.ds(at, 16), :]
             scl[s, pl.ds(at, 16), :] = scaled.astype(BF16)
             return kl + value * scaled
 
-        return lax.fori_loop(0, CH // 16, body, jnp.zeros((16, OB), F32))
+        return lax.fori_loop(
+            0, CH // 16, body, jnp.zeros((16, OB), F32), unroll=CH // 16
+        )
 
     def back_chunks(s, ks):
         for k in ks:
@@ -582,6 +592,8 @@
     for n in range(3):
         gv_copy(n).wait_recv()
     gv[me4] = gvs[...]
+    denominators(0)
+    denominators(1)
     for k in (2, 6):
         project(0, k)
     gather(0, 3)
@@ -682,7 +694,7 @@
         v((NZ, CH, OB), BF16), v((NZ, CH, OB), BF16), v(ring_b, BF16), v(ring_b, BF16),
         v((2, NZ, CH, OB), BF16), v((4 * GW, OUT_WIN), BF16), v((4 * GW, OUT_WIN), BF16),
         v((4, 8, GW), F32), v((8, GW), F32),
-        v((768, 128), F32), v((2, CH, OB), F32), v((2, CH, OB), BF16),
+        v((768, 128), F32), v((2, CH, OB), F32), v((2, CH, OB), F32), v((2, CH, OB), BF16),
         v((2, NZ, CH, OB), F32), v((2, *ring_b), BF16), v((2, *ring_b), BF16),
         v((2, 4, GW, CH), BF16), v((2, 4, GW, CH), BF16),
         v((32, GW, OB), F32), v((32, AW, 768), F32),

time: 78.2 us -> 77.6 us (level)
  no operation moved by 1% of the time
where the time goes in v5:
time: 77.6 us; the launch traced here: 77.5 us
  Pallas kernels  76.9 us (99%)
    pallas_call x1, Pallas kernels, per_device(): pl.pallas_call(kernel, out_shape=(jax.ShapeDtypeStruct((GW, 768), F32), j...  74.9 us
    pallas_call x1, Pallas kernels, per_device(): pl.pallas_call(finish, out_shape=(jax.ShapeDtypeStruct((GW, 768), F32), j...  1.96 us

profile of v5, /device:TPU:1, one launch (start us, length us, event | category | flops | bytes accessed | tf_op | source)
XLA Modules:
  0.0 77.5 jit_solution(7246303515849933758)
XLA Ops:
  0.6 74.9 %precondition.1 = (f32[96,768]{1,0:T(8,128)}, f32[144,384]{1,0:T(8,128)}, f32[8,128]{1,0:T(8,128)}) custom-call(bf16[512,768]{1,0:T(8,128)(2,1)} %acts_in.1, bf16[512,3072]{1,0:T(8,128)(2,1)} %grads_in.1, bf16[768,768]{1,0:T(8,128)(2,1)} %qa_in.1, bf16[96,3072]{1,0:T(8,128)(2,1)} %bitcast.1, f32[768]{0:T(1024)} %avals.1, f32[96]{0:T(128)} %gvals.1, ...), custom_call_target="tpu_custom_call" | custom-call | flops 5400000000 | bytes 8000000 | tf_op jit(solution)/shard_map/precondition/pallas_call | solution.py:715
  75.5 2.0 %finish.1 = (f32[96,768]{1,0:T(8,128)}, f32[24,768]{1,0:T(8,128)}, f32[96,384]{1,0:T(8,128)}) custom-call(f32[96,768]{1,0:T(8,128)} %get-tuple-element.6.total, f32[144,384]{1,0:T(8,128)} %get-tuple-element.7.gram, f32[8,128]{1,0:T(8,128)} %get-tuple-element.8.gain, f32[24,768]{1,0:T(8,128)} %afac.1, f32[96,384]{1,0:T(8,128)} %gfac.1), custom_call_target="tpu_custom_call" | custom-call | tf_op jit(solution)/shard_map/finish/pallas_call | solution.py:733

commit v6 on v5

--- a/solution.py
+++ b/solution.py
@@ -624,11 +624,11 @@
     back_chunks(1, (2, 6))
     back_step(1, 1, 0)
     back_step(1, 2, 1)
-    gram_own((1, 7, 0))
     kl_z()
     kl_y = kl_round(
         1, 4, lambda k: (y + k) % 4, lambda k: dev(y_=(y + k) % 4), kly, kly_s, kly_r
     )
+    gram_own((1, 7, 0))
     back_chunks(0, (1, 7, 0))
     back_step(0, 2, 0)
     back_step(0, 3, 1)

time: 77.6 us -> 77.6 us (level)
  no operation moved by 1% of the time
where the time goes in v6:
time: 77.6 us; the launch traced here: 77.5 us
  Pallas kernels  76.9 us (99%)
    pallas_call x1, Pallas kernels, per_device(): pl.pallas_call(kernel, out_shape=(jax.ShapeDtypeStruct((GW, 768), F32), j...  74.9 us
    pallas_call x1, Pallas kernels, per_device(): pl.pallas_call(finish, out_shape=(jax.ShapeDtypeStruct((GW, 768), F32), j...  1.96 us

profile of v6, /device:TPU:1, one launch (start us, length us, event | category | flops | bytes accessed | tf_op | source)
XLA Modules:
  0.0 77.5 jit_solution(1227190419367503741)
XLA Ops:
  0.6 74.9 %precondition.1 = (f32[96,768]{1,0:T(8,128)}, f32[144,384]{1,0:T(8,128)}, f32[8,128]{1,0:T(8,128)}) custom-call(bf16[512,768]{1,0:T(8,128)(2,1)} %acts_in.1, bf16[512,3072]{1,0:T(8,128)(2,1)} %grads_in.1, bf16[768,768]{1,0:T(8,128)(2,1)} %qa_in.1, bf16[96,3072]{1,0:T(8,128)(2,1)} %bitcast.1, f32[768]{0:T(1024)} %avals.1, f32[96]{0:T(128)} %gvals.1, ...), custom_call_target="tpu_custom_call" | custom-call | flops 5400000000 | bytes 8000000 | tf_op jit(solution)/shard_map/precondition/pallas_call | solution.py:715
  75.5 2.0 %finish.1 = (f32[96,768]{1,0:T(8,128)}, f32[24,768]{1,0:T(8,128)}, f32[96,384]{1,0:T(8,128)}) custom-call(f32[96,768]{1,0:T(8,128)} %get-tuple-element.6.total, f32[144,384]{1,0:T(8,128)} %get-tuple-element.7.gram, f32[8,128]{1,0:T(8,128)} %get-tuple-element.8.gain, f32[24,768]{1,0:T(8,128)} %afac.1, f32[96,384]{1,0:T(8,128)} %gfac.1), custom_call_target="tpu_custom_call" | custom-call | tf_op jit(solution)/shard_map/finish/pallas_call | solution.py:733
